TPU v7x, 32 devices: a whole 2x2x4 slice. The times are simulated.
32 devices in a mesh: slide: 8 (over z, x), band: 4 (over y, core).
Axes of the slice: x: 2, y: 2, z: 4, core: 2. Of those that a mesh axis runs over, the one named last changes fastest.
Arguments:
- queries: bfloat16 [16384, 1536], P(('slide', 'band')), parts along dimension 0, may hold values from -200 to 200
- keys: bfloat16 [16384, 1536], P(('slide', 'band')), parts along dimension 0, may hold values from -8 to 8
- values: bfloat16 [16384, 1536], P(('slide', 'band')), parts along dimension 0, may hold values from -6 to 6
- out_gain: float32 [1536], replicated, may hold values from 0.1 to 1.9
- out_weight: bfloat16 [1536, 1536], replicated, may hold values from -0.15625 to 0.15625
- adjacency: int32 [32, 2, 256], P(('slide', 'band')), parts along dimension 0, may hold values from 0 to 511, as said below
- send_counts: int32 [32, 2], P('slide'), parts along dimension 0, may hold values from 1 to 256
- coarse_index: int32 [1024], P(('slide', 'band')), parts along dimension 0, may hold values from 0 to 511, as said below
Outputs:
- context: bfloat16 [16384, 1536], P(('slide', 'band')), parts along dimension 0
There are 8 independent parts, one for each index of `slide`. A program takes and returns all parts, laid end to end along the dimension named above; an argument that names none is the same for every part. Nothing has to cross between parts.
Inputs may be any that keep to these rules, and one draw needn't show every extreme that they name: Within a band, adjacency side 0 lists rows from the first half of the band, side 1 from the second half; entries may repeat; entries at positions from the live count on are padding. `coarse_index`: entry r of a band's block lies in r * 16 to r * 16 + 15.
All inputs are finite; a program needn't handle non-finite values.
Results may differ from a plain program's by a relative error of at most 0.0085.
Values may be sent and summed in bfloat16 or wider, within the bound.
No kernel may reach another device: no remote copies, remote signals or barrier semaphores. Data moves between devices by JAX's collectives and lax.ppermute only.
A program may use at most 128 MiB of HBM per device.

v0:
```python
import jax
import jax.numpy as jnp
from jax import lax
from jax.sharding import PartitionSpec as P

H = 12
HD = 128


def shifted_2(block, axis, distance):
    devices = range(lax.axis_size(axis))
    route = [(i - distance, i) for i in devices if i - distance in devices]
    return lax.ppermute(block, axis, route)


def absorb(state, query_heads, key_rows, value_rows, live):
    high_old, total_old, accum_old = state
    count = key_rows.shape[0]
    key_heads = key_rows.reshape(count, H, HD)
    value_heads = value_rows.reshape(count, H, HD)
    scores = jnp.einsum(
        "qhd,khd->hqk", query_heads, key_heads, preferred_element_type=jnp.float32
    ) * (1.0 / HD**0.5)
    scores = jnp.where(live[None, None, :], scores, -1e30)
    high_new = jnp.maximum(high_old, jnp.max(scores, axis=2))
    factor = jnp.exp(high_old - high_new)
    weights = jnp.exp(scores - high_new[:, :, None])
    total_new = total_old * factor + jnp.sum(weights, axis=2)
    summed = jnp.einsum(
        "hqk,khd->qhd",
        weights.astype(jnp.bfloat16),
        value_heads,
        preferred_element_type=jnp.float32,
    )
    accum_new = accum_old * jnp.transpose(factor)[:, :, None] + summed
    return (high_new, total_new, accum_new)


def on_device(queries, keys, values, out_gain, out_weight, adjacency, send_counts, coarse_index):
    rows = queries.shape[0]
    bands = lax.axis_size("band")
    place = lax.axis_index("band")
    width = adjacency.shape[2]
    query_heads = queries.reshape(rows, H, HD)
    lower_rows = adjacency[0, 0]
    upper_rows = adjacency[0, 1]
    to_lower = jnp.stack([keys[lower_rows], values[lower_rows]], axis=1)
    to_upper = jnp.stack([keys[upper_rows], values[upper_rows]], axis=1)
    coarse = jnp.stack([keys[coarse_index], values[coarse_index]], axis=1)
    from_lower = shifted_2(to_upper, "band", 1)
    from_upper = shifted_2(to_lower, "band", -1)
    state = (
        jnp.full((H, rows), -1e30, jnp.float32),
        jnp.zeros((H, rows), jnp.float32),
        jnp.zeros((rows, H, HD), jnp.float32),
    )
    state = absorb(state, query_heads, keys, values, jnp.ones((rows,), jnp.bool_))
    lower_peer = jnp.maximum(place - 1, 0)
    upper_peer = jnp.minimum(place + 1, bands - 1)
    slots = jnp.arange(width, dtype=jnp.int32)
    lower_live = (slots < send_counts[lower_peer, 1]) & (place > 0)
    upper_live = (slots < send_counts[upper_peer, 0]) & (place < bands - 1)
    state = absorb(state, query_heads, from_lower[:, 0], from_lower[:, 1], lower_live)
    state = absorb(state, query_heads, from_upper[:, 0], from_upper[:, 1], upper_live)
    everything = lax.all_gather(coarse, "band", axis=0, tiled=True)
    state = absorb(
        state,
        query_heads,
        everything[:, 0],
        everything[:, 1],
        jnp.ones((everything.shape[0],), jnp.bool_),
    )
    totals = state[1]
    accum = state[2]
    attended = (accum / jnp.transpose(totals)[:, :, None]).reshape(rows, H * HD)
    center = jnp.mean(attended, axis=1, keepdims=True)
    shifted = attended - center
    spread = jnp.mean(shifted * shifted, axis=1, keepdims=True)
    normed = (shifted / jnp.sqrt(spread + 1e-05) * out_gain).astype(jnp.bfloat16)
    return jnp.dot(normed, out_weight, preferred_element_type=jnp.float32).astype(jnp.bfloat16)


def solution(mesh):
    in_specs = (
        P(("slide", "band"), None),
        P(("slide", "band"), None),
        P(("slide", "band"), None),
        P(),
        P(),
        P(("slide", "band"), None, None),
        P("slide", None),
        P(("slide", "band")),
    )
    out_specs = P(("slide", "band"), None)
    return jax.shard_map(
        on_device, mesh=mesh, in_specs=in_specs, out_specs=out_specs, check_vma=False
    )
```

profile of v0, /device:TPU:1, one launch (start us, length us, event | category | flops | bytes accessed | tf_op | source)
XLA Modules:
  0.0 113.5 jit_solution(8780664746098875045)
XLA Ops:
  0.0 0.8 compare_select_fusion.1
  0.8 0.0 copy-start.1
  0.8 4.6 %gather_fusion.2 = bf16[256,1536]{1,0:T(8,128)(2,1)} fusion(bf16[512,1536]{1,0:T(8,128)(2,1)} %param.9, s32[1024]{0:T(1024)S(1)} %pad_clamp_fusion.1), kind=kCustom, calls=%fused_computation.2 | custom fusion | bytes 1573888 | tf_op jit(solution)/shard_map/gather | solution.py:47
  5.4 2.1 %gather_fusion.3 = bf16[256,1536]{1,0:T(8,128)(2,1)} fusion(bf16[512,1536]{1,0:T(8,128)(2,1)S(1)} %copy-done.1, s32[1024]{0:T(1024)S(1)} %pad_clamp_fusion.1), kind=kCustom, calls=%fused_computation.3 | custom fusion | bytes 1573888 | tf_op jit(solution)/shard_map/gather | solution.py:47
  7.6 2.8 %pad_maximum_fusion.1 = bf16[256,2,1536]{2,0,1:T(8,128)(2,1)} fusion(bf16[256,1,1536]{2,0,1:T(8,128)(2,1)} %bitcast.182, bf16[256,1,1536]{2,0,1:T(8,128)(2,1)} %bitcast.181), kind=kLoop, calls=%fused_computation.56 | loop fusion | flops 786432 | bytes 3145728 | tf_op jit(solution)/shard_map/stack | solution.py:47
  10.4 2.0 %collective-permute-start.1 = (bf16[256,2,1536]{2,0,1:T(8,128)(2,1)}, bf16[256,2,1536]{2,0,1:T(8,128)(2,1)}, u32[]{:S(2)}, u32[]{:S(2)}) collective-permute-start(bf16[256,2,1536]{2,0,1:T(8,128)(2,1)} %pad_maximum_fusion.1), channel_id=1, source_target_pairs={{1,0},{2,1},{3,2},{5,4},{6,5},{7,6},{9,8},{10,9},{11,10},{13,12},{... | collective-permute-start | bytes 4718600 | tf_op jit(solution)/shard_map/ppermute | solution.py:13
  12.3 2.2 %gather_fusion = bf16[256,1536]{1,0:T(8,128)(2,1)} fusion(bf16[512,1536]{1,0:T(8,128)(2,1)S(1)} %copy-done, s32[1024]{0:T(1024)S(1)} %pad_clamp_fusion.2), kind=kCustom, calls=%fused_computation | custom fusion | bytes 1573888 | tf_op jit(solution)/shard_map/gather | solution.py:48
  14.5 2.1 %gather_fusion.1 = bf16[256,1536]{1,0:T(8,128)(2,1)} fusion(bf16[512,1536]{1,0:T(8,128)(2,1)S(1)} %copy-done.1, s32[1024]{0:T(1024)S(1)} %pad_clamp_fusion.2), kind=kCustom, calls=%fused_computation.1 | custom fusion | bytes 1573888 | tf_op jit(solution)/shard_map/gather | solution.py:48
  16.7 2.7 %pad_maximum_fusion = bf16[256,2,1536]{2,0,1:T(8,128)(2,1)} fusion(bf16[256,1,1536]{2,0,1:T(8,128)(2,1)} %bitcast.184, bf16[256,1,1536]{2,0,1:T(8,128)(2,1)} %bitcast.183), kind=kLoop, calls=%fused_computation.55 | loop fusion | flops 786432 | bytes 3145728 | tf_op jit(solution)/shard_map/stack | solution.py:48
  19.4 4.5 %collective-permute-start = (bf16[256,2,1536]{2,0,1:T(8,128)(2,1)}, bf16[256,2,1536]{2,0,1:T(8,128)(2,1)}, u32[]{:S(2)}, u32[]{:S(2)}) collective-permute-start(bf16[256,2,1536]{2,0,1:T(8,128)(2,1)} %pad_maximum_fusion), channel_id=1, source_target_pairs={{0,1},{1,2},{2,3},{4,5},{5,6},{6,7},{8,9},{9,10},{10,11},{12,13},{... | collective-permute-start | bytes 4718600 | tf_op jit(solution)/shard_map/ppermute | solution.py:13
  23.9 0.6 gather_fusion.4
  24.5 0.6 gather_fusion.5
  25.2 1.6 %copy.23 = bf16[512,1536]{0,1:T(8,128)(2,1)} copy(bf16[512,1536]{1,0:T(8,128)(2,1)S(1)} %copy-done) | data formatting | bytes 3145728 | tf_op args[1]
  26.8 0.7 copy.26
  27.5 1.7 %copy.22 = bf16[512,1536]{0,1:T(8,128)(2,1)S(1)} copy(bf16[512,1536]{1,0:T(8,128)(2,1)} %param.8) | data formatting | bytes 3145728 | tf_op args[0]
  29.2 16.4 %all_gather.3 = bf16[128,2,1536]{2,0,1:T(8,128)(2,1)S(1)} all-gather(bf16[32,2,1536]{2,0,1:T(8,128)(2,1)S(1)} %pad_maximum_fusion.2), channel_id=1, replica_groups=mesh['slide'=8,'band'=4] {'band'}, dimensions={0}, use_global_device_ids=true | all-gather | bytes 983040 | tf_op jit(solution)/shard_map/all_gather | solution.py:65
  45.6 0.8 fusion.59
  46.4 0.9 copy.38
  47.3 1.2 %copy.41 = bf16[128,1,1536]{0,2,1:T(8,128)(2,1)S(1)} copy(bf16[128,1,1536]{2,0,1:T(8,128)(2,1)} %get-tuple-element.16) | data formatting | bytes 786432 | tf_op jit(solution)/shard_map/slice | solution.py:70
  48.6 0.7 constant_dynamic-slice_fusion
  49.2 0.6 compare_and_fusion
  49.9 0.6 compare_and_fusion.1
  50.5 3.9 %bitcast_reduce_fusion.2 = (f32[12,512]{1,0:T(8,128)}, f32[12,128,512]{2,1,0:T(8,128)}) fusion(bf16[128,12,128]{0,2,1:T(8,128)(2,1)} %bitcast.186, bf16[512,12,128]{0,2,1:T(8,128)(2,1)S(1)} %bitcast.170), kind=kOutput, calls=%fused_computation.34 | convolution fusion | flops 202893312 | bytes 5136384 | tf_op jit(solution)/shard_map/qhd,khd->hqk/dot_general | solution.py:21
  54.4 7.0 %multiply_reduce_fusion = (f32[12,512]{1,0:T(8,128)}, f32[12,512,512]{1,2,0:T(8,128)}) fusion(bf16[512,12,128]{0,2,1:T(8,128)(2,1)S(1)} %bitcast.171, bf16[512,12,128]{0,2,1:T(8,128)(2,1)S(1)} %bitcast.177), kind=kOutput, calls=%fused_computation.7 | convolution fusion | flops 811591680 | bytes 15753216 | tf_op jit(solution)/shard_map/qhd,khd->hqk/dot_general | solution.py:21
  61.4 2.6 %fusion.57 = (bf16[256,1,1536]{2,0,1:T(8,128)(2,1)}, bf16[256,1,1536]{2,0,1:T(8,128)(2,1)}) fusion(bf16[256,2,1536]{2,0,1:T(8,128)(2,1)} %collective-permute-done.1), kind=kLoop, calls=%fused_computation.98 | loop fusion | bytes 3145728 | tf_op jit(solution)/shard_map/slice | solution.py:64
  64.0 2.3 %copy.33 = bf16[256,1,1536]{0,2,1:T(8,128)(2,1)} copy(bf16[256,1,1536]{2,0,1:T(8,128)(2,1)} %get-tuple-element.12) | data formatting | bytes 1572864 | tf_op jit(solution)/shard_map/slice | solution.py:64
  66.3 2.6 %fusion.58 = (bf16[256,1,1536]{2,0,1:T(8,128)(2,1)}, bf16[256,1,1536]{2,0,1:T(8,128)(2,1)}) fusion(bf16[256,2,1536]{2,0,1:T(8,128)(2,1)} %collective-permute-done), kind=kLoop, calls=%fused_computation.99 | loop fusion | bytes 3145728 | tf_op jit(solution)/shard_map/slice | solution.py:63
  69.0 2.3 %copy.28 = bf16[256,1,1536]{0,2,1:T(8,128)(2,1)} copy(bf16[256,1,1536]{2,0,1:T(8,128)(2,1)} %get-tuple-element.14) | data formatting | bytes 1572864 | tf_op jit(solution)/shard_map/slice | solution.py:63
  71.3 2.3 %copy.31 = bf16[256,1,1536]{0,2,1:T(8,128)(2,1)} copy(bf16[256,1,1536]{2,0,1:T(8,128)(2,1)} %get-tuple-element.13) | data formatting | bytes 1572864 | tf_op jit(solution)/shard_map/slice | solution.py:63
  73.6 5.4 %bitcast_reduce_fusion = (f32[12,512]{1,0:T(8,128)S(1)}, f32[12,256,512]{2,1,0:T(8,128)}) fusion(pred[256]{0:T(512)(128)(4,1)S(1)} %compare_and_fusion, bf16[256,12,128]{0,2,1:T(8,128)(2,1)} %bitcast.179, bf16[512,12,128]{0,2,1:T(8,128)(2,1)S(1)} %bitcast.172), kind=kOutput, calls=%fused_computation.12 | convolution fusion | flops 407365632 | bytes 8675584 | tf_op jit(solution)/shard_map/qhd,khd->hqk/dot_general | solution.py:21
  79.0 4.5 %bitcast_reduce_fusion.1 = (f32[12,512]{1,0:T(8,128)S(1)}, f32[12,256,512]{2,1,0:T(8,128)}) fusion(pred[256]{0:T(512)(128)(4,1)S(1)} %compare_and_fusion.1, bf16[256,12,128]{0,2,1:T(8,128)(2,1)S(1)} %bitcast.180, bf16[512,12,128]{0,2,1:T(8,128)(2,1)S(1)} %bitcast.173), kind=kOutput, calls=%fused_computation.15 | convolution fusion | flops 407365632 | bytes 8675584 | tf_op jit(solution)/shard_map/qhd,khd->hqk/dot_general | solution.py:21
  83.5 0.6 copy-done.15
  84.1 0.6 fusion.32
  84.7 2.4 %fusion.34 = f32[12,128,512]{2,1,0:T(8,128)} fusion(bf16[128,12,128]{0,2,1:T(8,128)(2,1)S(1)} %bitcast.185, f32[12,128,512]{2,1,0:T(8,128)S(1)} %copy-done.2, f32[12,512]{1,0:T(8,128)S(1)} %get-tuple-element.8), kind=kOutput, calls=%fused_computation.54 | convolution fusion | flops 203685888 | bytes 6709248 | tf_op jit(solution)/shard_map/hqk,khd->qhd/dot_general | solution.py:29
  87.1 2.1 %fusion = f32[12,512]{1,0:T(8,128)S(1)} fusion(f32[12,512,512]{1,2,0:T(8,128)S(1)} %bitcast.167, f32[12,512]{1,0:T(8,128)S(1)} %get-tuple-element.19), kind=kLoop, calls=%fused_computation.8 | loop fusion | flops 9431040 | bytes 12632064 | tf_op jit(solution)/shard_map/reduce_sum | solution.py:28
  89.2 4.2 %fusion.2 = f32[12,512,128]{1,2,0:T(8,128)} fusion(bf16[512,12,128]{0,2,1:T(8,128)(2,1)S(1)} %bitcast.176, f32[12,512,512]{1,2,0:T(8,128)S(1)} %bitcast.167, f32[12,512]{1,0:T(8,128)S(1)} %get-tuple-element.19), kind=kOutput, calls=%fused_computation.10 | convolution fusion | flops 814743552 | bytes 17326080 | tf_op jit(solution)/shard_map/hqk,khd->qhd/dot_general | solution.py:29
  93.4 2.4 %copy.36 = bf16[256,1,1536]{0,2,1:T(8,128)(2,1)} copy(bf16[256,1,1536]{2,0,1:T(8,128)(2,1)} %get-tuple-element.11) | data formatting | bytes 1572864 | tf_op jit(solution)/shard_map/slice | solution.py:64
  95.8 4.6 %fusion.14 = f32[12,128,512]{2,1,0:T(8,128)S(1)} fusion(bf16[256,12,128]{0,2,1:T(8,128)(2,1)S(1)} %bitcast.178, f32[12,256,512]{2,1,0:T(8,128)} %get-tuple-element.29, f32[12,512]{1,0:T(8,128)S(1)} %get-tuple-element.10, pred[256]{0:T(512)(128)(4,1)S(1)} %compare_and_fusion.1), kind=kOutput, calls=%fused_computation.26 | convolution fusion | flops 408944640 | bytes 10248448 | tf_op jit(solution)/shard_map/hqk,khd->qhd/dot_general | solution.py:29
  100.5 0.0 slice-start.7
  100.5 5.0 %fusion.8 = (f32[12,512]{1,0:T(8,128)S(1)}, f32[12,512]{1,0:T(8,128)S(1)}) fusion(f32[12,256,512]{2,1,0:T(8,128)S(1)} %bitcast.169, f32[12,512]{1,0:T(8,128)S(1)} %get-tuple-element.10, pred[256]{0:T(512)(128)(4,1)S(1)} %compare_and_fusion.1, f32[12,512]{1,0:T(8,128)S(1)} %get-tuple-element.9, f32[12,256,512]{2,1,0:T(8,128)} %get-tuple-element.27, ...), kind=kLoop, calls=%fused_computation.21 | loop fusion | flops 12570624 | bytes 12681728 | tf_op jit(solution)/shard_map/reduce_sum | solution.py:28
  105.7 0.2 copy-done.7
  105.9 0.1 copy-done.8
  106.0 2.5 %fusion.60 = (f32[512]{0:T(512)S(1)}, f32[512,12,128]{0,2,1:T(8,128)S(1)}) fusion(f32[512,12]{0,1:T(8,128)S(1)} %get-tuple-element.5, f32[12,128,512]{2,1,0:T(8,128)S(1)} %copy-done.6, f32[512,12]{0,1:T(8,128)S(1)} %get-tuple-element.7, bf16[256,12,128]{0,2,1:T(8,128)(2,1)S(1)} %bitcast.187, f32[12,256,512]{2,1,0:T(8,128)S(1)} %bitcast.175, ...), kind=kOutput, calls=%fused_computation.101 | convolution fusion | flops 416022016 | bytes 19810560 | tf_op jit(solution)/shard_map/hqk,khd->qhd/dot_general | solution.py:29
  108.5 0.0 copy-start.17
  108.5 0.4 multiply_reduce_fusion.1
  109.0 0.3 copy-done.17
  109.2 0.4 fusion.18
  109.7 3.8 %convolution_convert_fusion = bf16[512,1536]{1,0:T(8,128)(2,1)} fusion(bf16[512,1536]{0,1:T(8,128)(2,1)S(1)} %fusion.18, bf16[1536,1536]{1,0:T(8,128)(2,1)S(1)} %bitcast.193), kind=kOutput, calls=%fused_computation.51 | convolution fusion | flops 2416705536 | bytes 7864320 | tf_op jit(solution)/shard_map/dot_general | solution.py:80
  (66 shorter events, 0.2 us)
Async XLA Ops:
  0.8 4.7 %copy-start.1 = (bf16[512,1536]{1,0:T(8,128)(2,1)S(1)}, bf16[512,1536]{1,0:T(8,128)(2,1)}, u32[]{:S(2)}) copy-start(bf16[512,1536]{1,0:T(8,128)(2,1)} %param.10) | copy-start | bytes 4718596
  7.6 4.8 %copy-start = (bf16[512,1536]{1,0:T(8,128)(2,1)S(1)}, bf16[512,1536]{1,0:T(8,128)(2,1)}, u32[]{:S(2)}) copy-start(bf16[512,1536]{1,0:T(8,128)(2,1)} %param.9) | copy-start | bytes 4718596
  10.4 51.0 %collective-permute-start.1 = (bf16[256,2,1536]{2,0,1:T(8,128)(2,1)}, bf16[256,2,1536]{2,0,1:T(8,128)(2,1)}, u32[]{:S(2)}, u32[]{:S(2)}) collective-permute-start(bf16[256,2,1536]{2,0,1:T(8,128)(2,1)} %pad_maximum_fusion.1), channel_id=1, source_target_pairs={{1,0},{2,1},{3,2},{5,4},{6,5},{7,6},{9,8},{10,9},{11,10},{13,12},{... | collective-permute-start | bytes 4718600 | tf_op jit(solution)/shard_map/ppermute | solution.py:13
  16.7 7.2 %copy-start.19 = (s32[32]{0:T(128)S(1)}, s32[32]{0:T(128)}, u32[]{:S(2)}) copy-start(s32[32]{0:T(128)} %param.15) | copy-start | bytes 388
  19.4 47.0 %collective-permute-start = (bf16[256,2,1536]{2,0,1:T(8,128)(2,1)}, bf16[256,2,1536]{2,0,1:T(8,128)(2,1)}, u32[]{:S(2)}, u32[]{:S(2)}) collective-permute-start(bf16[256,2,1536]{2,0,1:T(8,128)(2,1)} %pad_maximum_fusion), channel_id=1, source_target_pairs={{0,1},{1,2},{2,3},{4,5},{5,6},{6,7},{8,9},{9,10},{10,11},{12,13},{... | collective-permute-start | bytes 4718600 | tf_op jit(solution)/shard_map/ppermute | solution.py:13
  27.5 21.1 %copy-start.18 = (s32[4,2]{0,1:T(2,128)S(1)}, s32[4,2]{0,1:T(2,128)}, u32[]{:S(2)}) copy-start(s32[4,2]{0,1:T(2,128)} %param.14) | copy-start | bytes 100
  48.6 5.9 %copy-start.3 = (bf16[512,1536]{0,1:T(8,128)(2,1)S(1)}, bf16[512,1536]{0,1:T(8,128)(2,1)}, u32[]{:S(2)}) copy-start(bf16[512,1536]{0,1:T(8,128)(2,1)} %copy.23) | copy-start | bytes 4718596
  73.6 5.4 %copy-start.5 = (bf16[256,1,1536]{0,2,1:T(8,128)(2,1)S(1)}, bf16[256,1,1536]{0,2,1:T(8,128)(2,1)}, u32[]{:S(2)}) copy-start(bf16[256,1,1536]{0,2,1:T(8,128)(2,1)} %copy.28) | copy-start | bytes 2359300
  73.6 13.5 %slice-start = ((s8[12582912]{0:T(1024)(128)(4,1)}), s8[4194304]{0:T(1024)(128)(4,1)S(1)}, s32[]{:S(2)}) async-start(s8[12582912]{0:T(1024)(128)(4,1)} %bitcast.166), calls=%async_computation | async-start | bytes 8388608
  79.0 4.5 %copy-start.13 = (f32[12,512]{1,0:T(8,128)}, f32[12,512]{1,0:T(8,128)S(1)}, u32[]{:S(2)}) copy-start(f32[12,512]{1,0:T(8,128)S(1)} %get-tuple-element.26) | copy-start | bytes 73732
  79.0 4.5 %copy-start.9 = (f32[12,512]{1,0:T(8,128)S(1)}, f32[12,512]{1,0:T(8,128)}, u32[]{:S(2)}) copy-start(f32[12,512]{1,0:T(8,128)} %get-tuple-element.24) | copy-start | bytes 73732
  79.0 4.5 %copy-start.11 = (f32[12,512]{1,0:T(8,128)S(1)}, f32[12,512]{1,0:T(8,128)}, u32[]{:S(2)}) copy-start(f32[12,512]{1,0:T(8,128)} %get-tuple-element.30) | copy-start | bytes 73732
  79.0 5.1 %copy-start.2 = (f32[12,128,512]{2,1,0:T(8,128)S(1)}, f32[12,128,512]{2,1,0:T(8,128)}, u32[]{:S(2)}) copy-start(f32[12,128,512]{2,1,0:T(8,128)} %get-tuple-element.25) | copy-start | bytes 9437188
  79.0 8.0 %slice-start.1 = ((s8[12582912]{0:T(1024)(128)(4,1)}), s8[4194304]{0:T(1024)(128)(4,1)S(1)}, s32[]{:S(2)}) async-start(s8[12582912]{0:T(1024)(128)(4,1)} %bitcast.166), calls=%async_computation.1 | async-start | bytes 8388608
  83.5 0.6 copy-start.15
  84.1 3.0 %slice-start.2 = ((s8[12582912]{0:T(1024)(128)(4,1)}), s8[4194304]{0:T(1024)(128)(4,1)S(1)}, s32[]{:S(2)}) async-start(s8[12582912]{0:T(1024)(128)(4,1)} %bitcast.166), calls=%async_computation.2 | async-start | bytes 8388608
  89.2 6.6 %copy-start.4 = (bf16[256,1,1536]{0,2,1:T(8,128)(2,1)S(1)}, bf16[256,1,1536]{0,2,1:T(8,128)(2,1)}, u32[]{:S(2)}) copy-start(bf16[256,1,1536]{0,2,1:T(8,128)(2,1)} %copy.31) | copy-start | bytes 2359300
  93.3 7.0 %slice-start.3 = ((s8[6291456]{0:T(1024)(128)(4,1)}), s8[2097152]{0:T(1024)(128)(4,1)S(1)}, s32[]{:S(2)}) async-start(s8[6291456]{0:T(1024)(128)(4,1)} %bitcast.168), calls=%async_computation.3 | async-start | bytes 4194304
  95.8 4.6 %slice-start.4 = ((s8[6291456]{0:T(1024)(128)(4,1)}), s8[4194304]{0:T(1024)(128)(4,1)S(1)}, s32[]{:S(2)}) async-start(s8[6291456]{0:T(1024)(128)(4,1)} %bitcast.168), calls=%async_computation.4 | async-start | bytes 8388608
  95.8 9.8 %slice-start.5 = ((s8[6291456]{0:T(1024)(128)(4,1)}), s8[4194304]{0:T(1024)(128)(4,1)S(1)}, s32[]{:S(2)}) async-start(s8[6291456]{0:T(1024)(128)(4,1)} %bitcast.174), calls=%async_computation.5 | async-start | bytes 8388608
  100.4 5.1 %copy-start.10 = (f32[12,512]{1,0:T(8,128)S(1)}, f32[12,512]{1,0:T(8,128)}, u32[]{:S(2)}) copy-start(f32[12,512]{1,0:T(8,128)} %get-tuple-element.24) | copy-start | bytes 73732
  100.4 5.1 %copy-start.12 = (f32[12,512]{1,0:T(8,128)S(1)}, f32[12,512]{1,0:T(8,128)}, u32[]{:S(2)}) copy-start(f32[12,512]{1,0:T(8,128)} %get-tuple-element.30) | copy-start | bytes 73732
  100.4 5.1 %copy-start.14 = (f32[12,512]{1,0:T(8,128)S(1)}, f32[12,512]{1,0:T(8,128)}, u32[]{:S(2)}) copy-start(f32[12,512]{1,0:T(8,128)} %copy-done.13) | copy-start | bytes 73732
  100.4 5.1 %copy-start.16 = (f32[12,512]{1,0:T(8,128)S(1)}, f32[12,512]{1,0:T(8,128)}, u32[]{:S(2)}) copy-start(f32[12,512]{1,0:T(8,128)} %copy-done.15) | copy-start | bytes 73732
  100.4 5.2 %slice-start.6 = ((s8[6291456]{0:T(1024)(128)(4,1)}), s8[2097152]{0:T(1024)(128)(4,1)S(1)}, s32[]{:S(2)}) async-start(s8[6291456]{0:T(1024)(128)(4,1)} %bitcast.174), calls=%async_computation.6 | async-start | bytes 4194304
  100.5 5.2 %copy-start.6 = (f32[12,128,512]{2,1,0:T(8,128)S(1)}, f32[12,128,512]{2,1,0:T(8,128)}, u32[]{:S(2)}) copy-start(f32[12,128,512]{2,1,0:T(8,128)} %fusion.34) | copy-start | bytes 9437188
  100.5 5.4 %copy-start.7 = (f32[12,512,128]{1,2,0:T(8,128)S(1)}, f32[12,512,128]{1,2,0:T(8,128)}, u32[]{:S(2)}) copy-start(f32[12,512,128]{1,2,0:T(8,128)} %fusion.2) | copy-start | bytes 9437188
  100.5 5.5 %copy-start.8 = (bf16[256,1,1536]{0,2,1:T(8,128)(2,1)S(1)}, bf16[256,1,1536]{0,2,1:T(8,128)(2,1)}, u32[]{:S(2)}) copy-start(bf16[256,1,1536]{0,2,1:T(8,128)(2,1)} %copy.36) | copy-start | bytes 2359300
  100.5 9.1 %slice-start.7 = ((s8[4718592]{0:T(1024)(128)(4,1)}), s8[4194304]{0:T(1024)(128)(4,1)S(1)}, s32[]{:S(2)}) async-start(s8[4718592]{0:T(1024)(128)(4,1)} %bitcast.192), calls=%async_computation.7 | async-start | bytes 8388608
  106.0 3.6 %slice-start.8 = ((s8[4718592]{0:T(1024)(128)(4,1)}), s8[524288]{0:T(1024)(128)(4,1)S(1)}, s32[]{:S(2)}) async-start(s8[4718592]{0:T(1024)(128)(4,1)} %bitcast.192), calls=%async_computation.8 | async-start | bytes 1048576
  108.5 0.7 copy-start.17
where the time goes:
time: 115 us; the launch traced here: 113 us
  matrix products  38.2 us (33%)
  local copies, waits for them, and re-layouts  35.9 us (31%)
  blocking collectives  16.4 us (14%)
  other arithmetic  16.1 us (14%)
  starting transfers between devices  6.43 us (6%)
    dot_general x4, matrix products, absorb(): jnp.einsum('qhd,khd->hqk', query_heads, key_heads, preferred_element_type...  20.8 us
    all_gather x1, blocking collectives, on_device(): everything = lax.all_gather(coarse, 'band', axis=0, tiled=True)  16.4 us
    dot_general x4, matrix products, absorb(): jnp.einsum('hqk,khd->qhd', weights.astype(jnp.bfloat16), value_heads, pre...  13.6 us
    reduce_sum x3, other arithmetic, absorb(): total_new = total_old * factor + jnp.sum(weights, axis=2)  7.7 us
    gather x2, local copies, waits for them, and re-layouts, on_device(): to_lower = jnp.stack([keys[lower_rows], values[lower_rows]], axis=1)  6.79 us
    ppermute x2, starting transfers between devices, shifted_2(): return lax.ppermute(block, axis, route)  6.43 us
    unnamed x61, local copies, waits for them, and re-layouts  5.28 us
    slice x2, local copies, waits for them, and re-layouts, on_device(): from_upper[:, 1]  5.07 us
  transfers between devices with their start and end apart: 2, of which 0 were waited for; matrix products, arithmetic and copies ran while one was open for 29% of the time, Pallas kernels for 0%

commit v1 on v0

v1 whole, which is shorter than its diff:
```python
import functools
import math

import jax
import jax.numpy as jnp
from jax import lax
from jax.experimental import pallas as pl
from jax.experimental.pallas import tpu as pltpu
from jax.sharding import PartitionSpec as P

H = 12
HD = 128
SCALE = math.log2(math.e) / math.sqrt(HD)
DEAD = -1e30
META_LANES = 384

VMEM = pltpu.VMEM
NT = (((1,), (1,)), ((), ()))


def dot(a, b):
    return jnp.dot(a, b, preferred_element_type=jnp.float32)


def dot_nt(a, b):
    return lax.dot_general(a, b, NT, preferred_element_type=jnp.float32)


def column(row):
    n = row.shape[1]
    shape = (n, n)
    diagonal = lax.broadcasted_iota(jnp.int32, shape, 0) == lax.broadcasted_iota(jnp.int32, shape, 1)
    return jnp.sum(jnp.where(diagonal, jnp.broadcast_to(row, shape), 0.0), axis=1, keepdims=True)


def log_mult(mult):
    return jnp.where(mult > 0.0, jnp.log2(jnp.maximum(mult, 1.0)), DEAD)


def coarse_kernel(index_ref, keys_ref, values_ref, out_ref):
    count = index_ref.shape[1]
    rows = keys_ref.shape[0]
    picked = column(index_ref[...].astype(jnp.float32))
    slots = lax.broadcasted_iota(jnp.int32, (count, rows), 1).astype(jnp.float32)
    choose = (picked == slots).astype(jnp.bfloat16)
    out_ref[0:count, :] = dot(choose, keys_ref[...]).astype(jnp.bfloat16)
    out_ref[count : 2 * count, :] = dot(choose, values_ref[...]).astype(jnp.bfloat16)


def multiplicity(adjacency_ref, counts_ref, side, base):
    width = adjacency_ref.shape[2]
    place = lax.axis_index("band")
    live = counts_ref[place, side]
    entries = adjacency_ref[0, pl.ds(side, 1), :].astype(jnp.float32) - base.astype(jnp.float32)
    shape = (width, width)
    slot = lax.broadcasted_iota(jnp.int32, shape, 0)
    row = lax.broadcasted_iota(jnp.int32, shape, 1).astype(jnp.float32)
    hits = jnp.where((column(entries) == row) & (slot < live), 1.0, 0.0)
    return jnp.sum(hits, axis=0, keepdims=True)


def boundary_kernel(adjacency_ref, counts_ref, keys_ref, values_ref, far_keys_ref, far_values_ref, near_mult_ref):
    width = adjacency_ref.shape[2]
    slots = far_keys_ref.shape[0]
    odd = lax.rem(lax.axis_index("band"), 2)
    base = pl.multiple_of(odd * width, width)
    near_mult = multiplicity(adjacency_ref, counts_ref, 1 - odd, (1 - odd) * width)
    near_mult_ref[...] = jnp.broadcast_to(near_mult, near_mult_ref.shape)
    mult = multiplicity(adjacency_ref, counts_ref, odd, base)
    present = (mult > 0.0).astype(jnp.bfloat16)
    square = (width, width)
    before = lax.broadcasted_iota(jnp.int32, square, 0) < lax.broadcasted_iota(jnp.int32, square, 1)
    order = dot(jnp.broadcast_to(present, (16, width)), before.astype(jnp.bfloat16))[0:1, :]
    place = jnp.where(mult > 0.0, order, -1.0)
    wanted = lax.broadcasted_iota(jnp.int32, (slots, width), 0)
    choose = (wanted.astype(jnp.float32) == place) & (wanted < slots - 1)
    choose = jnp.where(choose, 1.0, 0.0).astype(jnp.bfloat16)
    rows = pl.ds(base, width)
    slot_mult = dot_nt(jnp.broadcast_to(mult.astype(jnp.bfloat16), (16, width)), choose)[0:1, :]
    far_keys_ref[...] = dot(choose, keys_ref[rows, :]).astype(jnp.bfloat16)
    meta = jnp.concatenate([slot_mult, jnp.zeros((1, META_LANES - slots), jnp.float32)], axis=1)
    tail = slots - 16
    last = lax.broadcasted_iota(jnp.int32, (16, META_LANES), 0) == 15
    old = far_keys_ref[tail:slots, 0:META_LANES].astype(jnp.float32)
    far_keys_ref[tail:slots, 0:META_LANES] = jnp.where(last, meta, old).astype(jnp.bfloat16)
    far_values_ref[...] = dot(choose, values_ref[rows, :]).astype(jnp.bfloat16)


def head(h):
    return pl.ds(pl.multiple_of(h * HD, HD), HD)


def with_ones(rows):
    return jnp.concatenate([rows, jnp.ones_like(rows)], axis=1)


def put_column(ref, h, col):
    lane = lax.broadcasted_iota(jnp.int32, ref.shape, 1)
    ref[...] = jnp.where(lane == h, col, ref[...])


def get_column(ref, h):
    lane = lax.broadcasted_iota(jnp.int32, ref.shape, 1)
    return jnp.sum(jnp.where(lane == h, ref[...], 0.0), axis=1, keepdims=True)


def own_kernel(queries_ref, keys_ref, values_ref, high_ref, total_ref, accum_ref):
    high_ref[...] = jnp.zeros_like(high_ref)
    total_ref[...] = jnp.zeros_like(total_ref)

    def step(h, carry):
        cols = head(h)
        scores = dot_nt(queries_ref[:, cols], keys_ref[:, cols]) * SCALE
        high = jnp.max(scores, axis=1, keepdims=True)
        weights = jnp.exp2(scores - high).astype(jnp.bfloat16)
        summed = dot(weights, with_ones(values_ref[:, cols]))
        accum_ref[:, cols] = summed[:, :HD]
        put_column(high_ref, h, high)
        put_column(total_ref, h, summed[:, HD : HD + 1])
        return carry

    lax.fori_loop(0, H, step, 0, unroll=2)


def near_kernel(
    coarse_arrays, queries_ref, high_ref, total_ref, accum_ref, mult_ref, near_keys_ref, near_values_ref, *refs
):
    coarse_refs = refs[:coarse_arrays]
    high_out, total_out, accum_out, keys_ref, values_ref, sems = refs[coarse_arrays:]
    width = mult_ref.shape[1]
    odd = lax.rem(lax.axis_index("band"), 2)
    base = pl.multiple_of(odd * width, width)
    copies = [
        pltpu.make_async_copy(near_keys_ref.at[pl.ds(base, width)], keys_ref.at[pl.ds(0, width)], sems.at[0]),
        pltpu.make_async_copy(near_values_ref.at[pl.ds(base, width)], values_ref.at[pl.ds(0, width)], sems.at[1]),
    ]
    count = coarse_refs[0].shape[0] // 2
    for i, ref in enumerate(coarse_refs):
        to = pl.ds(width + i * count, count)
        copies.append(pltpu.make_async_copy(ref.at[pl.ds(0, count)], keys_ref.at[to], sems.at[2 + 2 * i]))
        copies.append(pltpu.make_async_copy(ref.at[pl.ds(count, count)], values_ref.at[to], sems.at[3 + 2 * i]))
    for copy in copies:
        copy.start()
    coarse = keys_ref.shape[0] - width
    bias = jnp.concatenate([log_mult(mult_ref[0:1, :]), jnp.zeros((1, coarse), jnp.float32)], axis=1)
    high_out[...] = jnp.zeros_like(high_out)
    total_out[...] = jnp.zeros_like(total_out)
    for copy in copies:
        copy.wait()

    def step(h, carry):
        cols = head(h)
        scores = dot_nt(queries_ref[:, cols], keys_ref[:, cols]) * SCALE + bias
        old = get_column(high_ref, h)
        high = jnp.maximum(old, jnp.max(scores, axis=1, keepdims=True))
        factor = jnp.exp2(old - high)
        weights = jnp.exp2(scores - high).astype(jnp.bfloat16)
        summed = dot(weights, with_ones(values_ref[:, cols]))
        accum_out[:, cols] = accum_ref[:, cols] * factor + summed[:, :HD]
        put_column(high_out, h, high)
        put_column(total_out, h, get_column(total_ref, h) * factor + summed[:, HD : HD + 1])
        return carry

    lax.fori_loop(0, H, step, 0, unroll=2)


def far_kernel(queries_ref, high_ref, total_ref, accum_ref, far_keys_ref, accum_out, weights_out):
    slots = far_keys_ref.shape[0]
    meta = far_keys_ref[slots - 16 : slots, 0:META_LANES].astype(jnp.float32)
    last = lax.broadcasted_iota(jnp.int32, meta.shape, 0) == 15
    mult = jnp.sum(jnp.where(last, meta, 0.0), axis=0, keepdims=True)
    bias = log_mult(mult[:, 0:slots])

    def step(h, carry):
        cols = head(h)
        scores = dot_nt(queries_ref[:, cols], far_keys_ref[:, cols]) * SCALE + bias
        old = get_column(high_ref, h)
        high = jnp.maximum(old, jnp.max(scores, axis=1, keepdims=True))
        factor = jnp.exp2(old - high)
        weights = jnp.exp2(scores - high)
        total = get_column(total_ref, h) * factor + jnp.sum(weights, axis=1, keepdims=True)
        inverse = 1.0 / total
        accum_out[:, cols] = accum_ref[:, cols] * (factor * inverse)
        weights_out[h] = (weights * inverse).astype(jnp.bfloat16)
        return carry

    lax.fori_loop(0, H, step, 0, unroll=2)


def project_kernel(accum_ref, weights_ref, far_values_ref, gain_ref, matrix_ref, out_ref, normed_ref):
    rows, width = accum_ref.shape
    chunk = 256
    for start in range(0, rows, chunk):
        part = pl.ds(start, chunk)
        heads = [
            accum_ref[part, h * HD : (h + 1) * HD]
            + dot(weights_ref[h, part, :], far_values_ref[:, h * HD : (h + 1) * HD])
            for h in range(H)
        ]
        center = jnp.sum(functools.reduce(jnp.add, heads), axis=1, keepdims=True) * (1.0 / width)
        heads = [x - center for x in heads]
        square = functools.reduce(jnp.add, [x * x for x in heads])
        spread = jnp.sum(square, axis=1, keepdims=True) * (1.0 / width)
        inverse = lax.rsqrt(spread + 1e-05)
        for h, x in enumerate(heads):
            cols = slice(h * HD, (h + 1) * HD)
            normed_ref[part, cols] = (x * inverse * gain_ref[:, cols]).astype(jnp.bfloat16)
        out_ref[part, :] = dot(normed_ref[part, :], matrix_ref[...]).astype(jnp.bfloat16)


def spec(space=VMEM):
    return pl.BlockSpec(memory_space=space)


def call(kernel, ins, outs, scratch=(), limit=24, cost=None):
    flops, nbytes, exps = cost
    return pl.pallas_call(
        kernel,
        in_specs=[spec(s) for _, s in ins],
        out_specs=tuple(spec() for _ in outs),
        out_shape=tuple(
            pltpu.VMEM(shape, dtype) if keep else jax.ShapeDtypeStruct(shape, dtype) for shape, dtype, keep in outs
        ),
        scratch_shapes=list(scratch),
        compiler_params=pltpu.CompilerParams(vmem_limit_bytes=limit << 20),
        cost_estimate=pl.CostEstimate(flops=flops, bytes_accessed=nbytes, transcendentals=exps),
    )(*[x for x, _ in ins])


def on_device(queries, keys, values, out_gain, out_weight, adjacency, send_counts, coarse_index):
    rows, width = queries.shape
    bands = lax.axis_size("band")
    half = adjacency.shape[2]
    count = coarse_index.shape[0]
    slots = half + 16
    bf16, f32 = jnp.bfloat16, jnp.float32
    smem = pltpu.SMEM

    def swap(block, mask):
        return lax.ppermute(block, "band", [(i, i ^ mask) for i in range(bands)])

    def far(block):
        up = [(i, i + 1) for i in range(1, bands - 1, 2)]
        return lax.ppermute(block, "band", up + [(j, i) for i, j in up])

    (coarse,) = call(
        coarse_kernel,
        [(coarse_index.reshape(1, count), VMEM), (keys, VMEM), (values, VMEM)],
        [((2 * count, width), bf16, False)],
        cost=(4 * count * rows * width, 4 * rows * width, 0),
    )
    pieces = [coarse]
    masks = [1] if bands == 2 else [bands - 1] + [1 << i for i in range(bands.bit_length() - 2)]
    for mask in masks:
        pieces = pieces + [swap(piece, mask) for piece in pieces]
    near_keys, near_values = swap(keys, 1), swap(values, 1)
    far_keys, far_values, near_mult = call(
        boundary_kernel,
        [(adjacency, VMEM), (send_counts, smem), (keys, VMEM), (values, VMEM)],
        [((slots, width), bf16, False), ((slots, width), bf16, False), ((8, half), f32, False)],
        cost=(4 * slots * half * width, 4 * rows * width, 0),
    )
    far_keys, far_values = far(far_keys), far(far_values)
    near_mult = swap(near_mult, 1)

    state = [((rows, HD), f32, True), ((rows, HD), f32, True), ((rows, width), f32, True)]
    high, total, accum = call(
        own_kernel,
        [(queries, VMEM), (keys, VMEM), (values, VMEM)],
        state,
        cost=(4 * rows * rows * width, 6 * rows * width, H * rows * rows),
    )
    seen = half + len(pieces) * count
    high, total, accum = call(
        functools.partial(near_kernel, len(pieces)),
        [(queries, VMEM), (high, VMEM), (total, VMEM), (accum, VMEM), (near_mult, VMEM)]
        + [(x, pl.ANY) for x in [near_keys, near_values] + pieces],
        state,
        scratch=[
            pltpu.VMEM((seen, width), bf16),
            pltpu.VMEM((seen, width), bf16),
            pltpu.SemaphoreType.DMA((2 + 2 * len(pieces),)),
        ],
        cost=(4 * rows * seen * width, 2 * rows * width, H * rows * seen),
    )
    accum, weights = call(
        far_kernel,
        [(queries, VMEM), (high, VMEM), (total, VMEM), (accum, VMEM), (far_keys, VMEM)],
        [((rows, width), f32, True), ((H, rows, slots), bf16, True)],
        cost=(2 * rows * slots * width, 2 * rows * width, H * rows * slots),
    )
    (context,) = call(
        project_kernel,
        [
            (accum, VMEM),
            (weights, VMEM),
            (far_values, VMEM),
            (out_gain.reshape(1, width), VMEM),
            (out_weight, VMEM),
        ],
        [((rows, width), bf16, False)],
        scratch=[pltpu.VMEM((rows, width), bf16)],
        cost=(2 * rows * width * (slots + width), 2 * width * width, 0),
    )
    return context


def solution(mesh):
    in_specs = (
        P(("slide", "band"), None),
        P(("slide", "band"), None),
        P(("slide", "band"), None),
        P(),
        P(),
        P(("slide", "band"), None, None),
        P("slide", None),
        P(("slide", "band")),
    )
    out_specs = P(("slide", "band"), None)
    return jax.shard_map(
        on_device, mesh=mesh, in_specs=in_specs, out_specs=out_specs, check_vma=False
    )
```

time: 115 us -> 62 us (0.54)
  matrix products: 38.2 us -> 0 us
  local copies, waits for them, and re-layouts: 35.9 us -> 4.3 us
  Pallas kernels: 0 us -> 27.8 us
  waiting for transfers between devices: 0.01 us -> 20.3 us
  blocking collectives: 16.4 us -> 0 us
  other arithmetic: 16.1 us -> 0.01 us
  starting transfers between devices: 6.43 us -> 8.91 us
    dot_general x9 -> x0, matrix products: 38.2 us -> none  [the longest x4 20.8 us: absorb(): jnp.einsum('qhd,khd->hqk', query_heads, key_heads, preferred_element_type...]
    pallas_call x0 -> x6, Pallas kernels: none -> 27.8 us  [call(): pl.pallas_call(kernel, in_specs=[spec(s) for _, s in ins], out_specs=tupl...]
    ppermute x2 -> x8, waiting for transfers between devices: 0.01 us -> 20.3 us  [the longest x6 20.3 us: swap(): return lax.ppermute(block, 'band', [(i, i ^ mask) for i in range(bands)])]
    slice x9 -> x0, local copies, waits for them, and re-layouts: 17.5 us -> none  [the longest x2 5.07 us: on_device(): from_upper[:, 1]]
    all_gather x1 -> x0, blocking collectives: 16.4 us -> none  [on_device(): everything = lax.all_gather(coarse, 'band', axis=0, tiled=True)]
    gather x6 -> x0, local copies, waits for them, and re-layouts: 12.4 us -> none  [the longest x2 6.79 us: on_device(): to_lower = jnp.stack([keys[lower_rows], values[lower_rows]], axis=1)]
    reduce_sum x4 -> x0, other arithmetic: 8.11 us -> none  [the longest x3 7.7 us: absorb(): total_new = total_old * factor + jnp.sum(weights, axis=2)]
    another operation x3 -> x0, other arithmetic: 5.49 us -> none  [the longest x1 2.78 us: on_device(): to_lower = jnp.stack([keys[lower_rows], values[lower_rows]], axis=1)]
  transfers between devices with their start and end apart: 2 -> 8, of which waited for: 0 -> 3; matrix products, arithmetic and copies ran while one was open for 29% -> 1% of each run, Pallas kernels for 0% -> 35%
where the time goes in v1:
time: 62 us; the launch traced here: 61.5 us
  Pallas kernels  27.8 us (45%)
  waiting for transfers between devices  20.3 us (33%)
  starting transfers between devices  8.91 us (14%)
  local copies, waits for them, and re-layouts  4.3 us (7%)
    pallas_call x6, Pallas kernels, call(): pl.pallas_call(kernel, in_specs=[spec(s) for _, s in ins], out_specs=tupl...  27.8 us
    ppermute x6, waiting for transfers between devices, swap(): return lax.ppermute(block, 'band', [(i, i ^ mask) for i in range(bands)])  20.3 us
    ppermute x2, starting transfers between devices, far(): return lax.ppermute(block, 'band', up + [(j, i) for i, j in up])  6.46 us
    unnamed x19, local copies, waits for them, and re-layouts  4.3 us
    ppermute x6, starting transfers between devices, swap(): return lax.ppermute(block, 'band', [(i, i ^ mask) for i in range(bands)])  2.46 us
  transfers between devices with their start and end apart: 8, of which 3 were waited for; matrix products, arithmetic and copies ran while one was open for 1% of the time, Pallas kernels for 35%

profile of v1, /device:TPU:1, one launch (start us, length us, event | category | flops | bytes accessed | tf_op | source)
XLA Modules:
  0.0 61.5 jit_solution(6040040090660409322)
XLA Ops:
  0.0 0.1 collective-permute-start.1
  0.1 0.5 collective-permute-start.2
  0.5 0.8 %copy.9.counts_ref = s32[4,2]{1,0:T(4,128)S(1)} copy(s32[4,2]{0,1:T(2,128)} %param.14) | data formatting | bytes 64 | tf_op args[6]
  1.3 0.0 copy-start
  1.3 1.4 %copy-done = bf16[512,1536]{1,0:T(8,128)(2,1)S(1)} copy-done((bf16[512,1536]{1,0:T(8,128)(2,1)S(1)}, bf16[512,1536]{1,0:T(8,128)(2,1)}, u32[]{:S(2)}) %copy-start) | copy-done | bytes 1572888
  2.7 0.0 copy-start.2
  2.7 1.4 %copy-done.2 = bf16[512,1536]{1,0:T(8,128)(2,1)S(1)} copy-done((bf16[512,1536]{1,0:T(8,128)(2,1)S(1)}, bf16[512,1536]{1,0:T(8,128)(2,1)}, u32[]{:S(2)}) %copy-start.2) | copy-done | bytes 1572888
  4.1 0.0 copy-start.4
  4.1 0.7 %copy-done.4 = s32[1,2,256]{2,1,0:T(2,128)S(1)} copy-done((s32[1,2,256]{2,1,0:T(2,128)S(1)}, s32[1,2,256]{2,1,0:T(2,128)}, u32[]{:S(2)}) %copy-start.4) | copy-done | bytes 2072
  4.8 0.0 copy-start.5
  4.8 1.5 %shard_map.83 = (bf16[272,1536]{1,0:T(8,128)(2,1)S(1)}, bf16[272,1536]{1,0:T(8,128)(2,1)S(1)}, f32[8,256]{1,0:T(8,128)S(1)}) custom-call(s32[1,2,256]{2,1,0:T(2,128)S(1)} %copy-done.4, s32[4,2]{1,0:T(4,128)S(1)} %copy.9.counts_ref, bf16[512,1536]{1,0:T(8,128)(2,1)S(1)} %copy-done, bf16[512,1536]{1,0:T(8,128)(2,1)S(1)} %copy-done.2), custom_call_target="tpu_custom_call" | custom-call | flops 427819008 | bytes 3145728 | tf_op jit(solution)/shard_map/pallas_call | solution.py:217
  6.2 4.5 %collective-permute-start.6 = (bf16[272,1536]{1,0:T(8,128)(2,1)S(1)}, bf16[272,1536]{1,0:T(8,128)(2,1)S(1)}, u32[]{:S(2)}, u32[]{:S(2)}) collective-permute-start(bf16[272,1536]{1,0:T(8,128)(2,1)S(1)} %get-tuple-element.23), channel_id=1, source_target_pairs={{1,2},{2,1},{5,6},{6,5},{9,10},{10,9},{13,14},{14,13},{17,18},{18,... | collective-permute-start | bytes 2506760 | tf_op jit(solution)/shard_map/ppermute | solution.py:244
  10.8 1.9 %collective-permute-start.7 = (bf16[272,1536]{1,0:T(8,128)(2,1)S(1)}, bf16[272,1536]{1,0:T(8,128)(2,1)S(1)}, u32[]{:S(2)}, u32[]{:S(2)}) collective-permute-start(bf16[272,1536]{1,0:T(8,128)(2,1)S(1)} %get-tuple-element.26), channel_id=1, source_target_pairs={{1,2},{2,1},{5,6},{6,5},{9,10},{10,9},{13,14},{14,13},{17,18},{18,... | collective-permute-start | bytes 2506760 | tf_op jit(solution)/shard_map/ppermute | solution.py:244
  12.7 0.1 collective-permute-start
  12.8 0.0 copy-done.5
  12.8 0.0 copy-start.6
  12.8 0.0 copy-start.1
  12.8 0.0 copy-start.3
  12.8 0.7 %shard_map.84.refs_0_ = bf16[64,1536]{1,0:T(8,128)(2,1)S(1)} custom-call(s32[1,32]{1,0:T(1,128)S(1)} %bitcast.3, bf16[512,1536]{1,0:T(8,128)(2,1)S(1)} %copy-done, bf16[512,1536]{1,0:T(8,128)(2,1)S(1)} %copy-done.2), custom_call_target="tpu_custom_call" | custom-call | flops 100663296 | bytes 3145728 | tf_op jit(solution)/shard_map/pallas_call | solution.py:217
  13.5 0.4 collective-permute-done.mult_ref
  13.9 1.7 %collective-permute-start.3 = (bf16[64,1536]{1,0:T(8,128)(2,1)S(1)}, bf16[64,1536]{1,0:T(8,128)(2,1)S(1)}, u32[]{:S(2)}, u32[]{:S(2)}) collective-permute-start(bf16[64,1536]{1,0:T(8,128)(2,1)S(1)} %shard_map.84.refs_0_), channel_id=1, source_target_pairs={{0,3},{1,2},{2,1},{3,0},{4,7},{5,6},{6,5},{7,4},{8,11},{9,10},{10,... | collective-permute-start | bytes 589832 | tf_op jit(solution)/shard_map/ppermute | solution.py:240
  15.7 18.5 %collective-permute-done.3.refs_1_ = bf16[64,1536]{1,0:T(8,128)(2,1)S(1)} collective-permute-done((bf16[64,1536]{1,0:T(8,128)(2,1)S(1)}, bf16[64,1536]{1,0:T(8,128)(2,1)S(1)}, u32[]{:S(2)}, u32[]{:S(2)}) %collective-permute-start.3) | collective-permute-done | bytes 196640 | tf_op jit(solution)/shard_map/ppermute | solution.py:240
  34.1 0.0 collective-permute-start.4
  34.1 1.4 %collective-permute-done.4.refs_2_ = bf16[64,1536]{1,0:T(8,128)(2,1)S(1)} collective-permute-done((bf16[64,1536]{1,0:T(8,128)(2,1)S(1)}, bf16[64,1536]{1,0:T(8,128)(2,1)S(1)}, u32[]{:S(2)}, u32[]{:S(2)}) %collective-permute-start.4) | collective-permute-done | bytes 196640 | tf_op jit(solution)/shard_map/ppermute | solution.py:240
  35.6 0.1 collective-permute-start.5
  35.7 0.0 copy-done.6
  35.7 0.0 copy-done.1
  35.7 0.0 copy-done.3
  35.7 0.0 slice-start
  35.8 7.0 %shard_map.82 = (f32[512,128]{1,0:T(8,128)S(1)}, f32[512,128]{1,0:T(8,128)S(1)}, f32[512,1536]{1,0:T(8,128)S(1)}) custom-call(bf16[512,1536]{1,0:T(8,128)(2,1)S(1)} %copy-done.3, bf16[512,1536]{1,0:T(8,128)(2,1)S(1)} %copy-done.1, bf16[512,1536]{1,0:T(8,128)(2,1)S(1)} %copy-done.2), custom_call_target="tpu_custom_call" | custom-call | flops 1610612736 | bytes 4718592 | tf_op jit(solution)/shard_map/pallas_call | solution.py:217
  42.7 0.0 collective-permute-done.5.refs_3_
  42.8 0.0 collective-permute-done.1.near_keys_ref
  42.8 0.0 collective-permute-done.2.near_values_ref
  42.8 0.0 slice-start.1
  42.8 7.7 %shard_map.85 = (f32[512,128]{1,0:T(8,128)S(1)}, f32[512,128]{1,0:T(8,128)S(1)}, f32[512,1536]{1,0:T(8,128)S(1)}) custom-call(bf16[512,1536]{1,0:T(8,128)(2,1)S(1)} %copy-done.3, f32[512,128]{1,0:T(8,128)S(1)} %get-tuple-element.16.high_ref, f32[512,128]{1,0:T(8,128)S(1)} %get-tuple-element.17.total_ref, f32[512,1536]{1,0:T(8,128)S(1)} %get-tuple-element.18.accum_ref, ...), custom_call_target="tpu_custom_call" | custom-call | flops 1207959552 | bytes 1572864 | tf_op jit(solution)/shard_map/pallas_call | solution.py:217
  50.5 0.0 collective-permute-done.6.far_keys_ref
  50.6 4.9 %shard_map.86 = (f32[512,1536]{1,0:T(8,128)S(1)}, bf16[12,512,272]{2,1,0:T(8,128)(2,1)S(1)}) custom-call(bf16[512,1536]{1,0:T(8,128)(2,1)S(1)} %copy-done.3, f32[512,128]{1,0:T(8,128)S(1)} %get-tuple-element.20.high_ref, f32[512,128]{1,0:T(8,128)S(1)} %get-tuple-element.21.total_ref, f32[512,1536]{1,0:T(8,128)S(1)} %get-tuple-element.22.accum_ref, ...), custom_call_target="tpu_custom_call" | custom-call | flops 427819008 | bytes 1572864 | tf_op jit(solution)/shard_map/pallas_call | solution.py:217
  55.5 0.0 collective-permute-done.7.far_values_ref
  55.5 0.0 slice-done
  55.5 0.0 slice-done.1
  55.5 6.0 %shard_map.87 = bf16[512,1536]{1,0:T(8,128)(2,1)} custom-call(f32[512,1536]{1,0:T(8,128)S(1)} %get-tuple-element.24.accum_ref, bf16[12,512,272]{2,1,0:T(8,128)(2,1)S(1)} %get-tuple-element.25.weights_ref, bf16[272,1536]{1,0:T(8,128)(2,1)S(1)} %collective-permute-done.7.far_values_ref, f32[1,1536]{1,0:T(1,128)S(1)} %reshape.7.gain_ref, ...), custom_call_target="tpu_custom_call" | custom-call | flops 2843738112 | bytes 4718592 | tf_op jit(solution)/shard_map/pallas_call | solution.py:217
  (2 shorter events, 0.0 us)
Async XLA Ops:
  0.0 42.8 %collective-permute-start.1 = (bf16[512,1536]{1,0:T(8,128)(2,1)}, bf16[512,1536]{1,0:T(8,128)(2,1)S(1)}, u32[]{:S(2)}, u32[]{:S(2)}) collective-permute-start(bf16[512,1536]{1,0:T(8,128)(2,1)} %keys_ref.5), channel_id=1, source_target_pairs={{0,1},{1,0},{2,3},{3,2},{4,5},{5,4},{6,7},{7,6},{8,9},{9,8},{10,11... | collective-permute-start | bytes 4718600 | tf_op jit(solution)/shard_map/ppermute | solution.py:240
  0.1 42.7 %collective-permute-start.2 = (bf16[512,1536]{1,0:T(8,128)(2,1)}, bf16[512,1536]{1,0:T(8,128)(2,1)S(1)}, u32[]{:S(2)}, u32[]{:S(2)}) collective-permute-start(bf16[512,1536]{1,0:T(8,128)(2,1)} %values_ref.5), channel_id=1, source_target_pairs={{0,1},{1,0},{2,3},{3,2},{4,5},{5,4},{6,7},{7,6},{8,9},{9,8},{10,11... | collective-permute-start | bytes 4718600 | tf_op jit(solution)/shard_map/ppermute | solution.py:240
  1.3 1.4 %copy-start = (bf16[512,1536]{1,0:T(8,128)(2,1)S(1)}, bf16[512,1536]{1,0:T(8,128)(2,1)}, u32[]{:S(2)}) copy-start(bf16[512,1536]{1,0:T(8,128)(2,1)} %keys_ref.5) | copy-start | bytes 4718596
  2.7 1.4 %copy-start.2 = (bf16[512,1536]{1,0:T(8,128)(2,1)S(1)}, bf16[512,1536]{1,0:T(8,128)(2,1)}, u32[]{:S(2)}) copy-start(bf16[512,1536]{1,0:T(8,128)(2,1)} %values_ref.5) | copy-start | bytes 4718596
  4.1 0.7 %copy-start.4 = (s32[1,2,256]{2,1,0:T(2,128)S(1)}, s32[1,2,256]{2,1,0:T(2,128)}, u32[]{:S(2)}) copy-start(s32[1,2,256]{2,1,0:T(2,128)} %adjacency_ref.1) | copy-start | bytes 6148
  4.8 8.0 %copy-start.5 = (s32[32]{0:T(128)S(1)}, s32[32]{0:T(128)}, u32[]{:S(2)}) copy-start(s32[32]{0:T(128)} %param.15) | copy-start | bytes 388
  6.2 44.3 %collective-permute-start.6 = (bf16[272,1536]{1,0:T(8,128)(2,1)S(1)}, bf16[272,1536]{1,0:T(8,128)(2,1)S(1)}, u32[]{:S(2)}, u32[]{:S(2)}) collective-permute-start(bf16[272,1536]{1,0:T(8,128)(2,1)S(1)} %get-tuple-element.23), channel_id=1, source_target_pairs={{1,2},{2,1},{5,6},{6,5},{9,10},{10,9},{13,14},{14,13},{17,18},{18,... | collective-permute-start | bytes 2506760 | tf_op jit(solution)/shard_map/ppermute | solution.py:244
  10.8 44.7 %collective-permute-start.7 = (bf16[272,1536]{1,0:T(8,128)(2,1)S(1)}, bf16[272,1536]{1,0:T(8,128)(2,1)S(1)}, u32[]{:S(2)}, u32[]{:S(2)}) collective-permute-start(bf16[272,1536]{1,0:T(8,128)(2,1)S(1)} %get-tuple-element.26), channel_id=1, source_target_pairs={{1,2},{2,1},{5,6},{6,5},{9,10},{10,9},{13,14},{14,13},{17,18},{18,... | collective-permute-start | bytes 2506760 | tf_op jit(solution)/shard_map/ppermute | solution.py:244
  12.7 1.2 %collective-permute-start = (f32[8,256]{1,0:T(8,128)S(1)}, f32[8,256]{1,0:T(8,128)S(1)}, u32[]{:S(2)}, u32[]{:S(2)}) collective-permute-start(f32[8,256]{1,0:T(8,128)S(1)} %get-tuple-element.19), channel_id=1, source_target_pairs={{0,1},{1,0},{2,3},{3,2},{4,5},{5,4},{6,7},{7,6},{8,9},{9,8},{10,11... | collective-permute-start | bytes 24584 | tf_op jit(solution)/shard_map/ppermute | solution.py:240
  12.8 22.9 %copy-start.6 = (f32[1536]{0:T(1024)S(1)}, f32[1536]{0:T(1024)}, u32[]{:S(2)}) copy-start(f32[1536]{0:T(1024)} %param.11) | copy-start | bytes 18436
  12.8 22.9 %copy-start.1 = (bf16[512,1536]{1,0:T(8,128)(2,1)S(1)}, bf16[512,1536]{1,0:T(8,128)(2,1)}, u32[]{:S(2)}) copy-start(bf16[512,1536]{1,0:T(8,128)(2,1)} %keys_ref.5) | copy-start | bytes 4718596
  12.8 22.9 %copy-start.3 = (bf16[512,1536]{1,0:T(8,128)(2,1)S(1)}, bf16[512,1536]{1,0:T(8,128)(2,1)}, u32[]{:S(2)}) copy-start(bf16[512,1536]{1,0:T(8,128)(2,1)} %queries_ref.5) | copy-start | bytes 4718596
  13.9 20.2 %collective-permute-start.3 = (bf16[64,1536]{1,0:T(8,128)(2,1)S(1)}, bf16[64,1536]{1,0:T(8,128)(2,1)S(1)}, u32[]{:S(2)}, u32[]{:S(2)}) collective-permute-start(bf16[64,1536]{1,0:T(8,128)(2,1)S(1)} %shard_map.84.refs_0_), channel_id=1, source_target_pairs={{0,3},{1,2},{2,1},{3,0},{4,7},{5,6},{6,5},{7,4},{8,11},{9,10},{10,... | collective-permute-start | bytes 589832 | tf_op jit(solution)/shard_map/ppermute | solution.py:240
  34.1 1.4 %collective-permute-start.4 = (bf16[64,1536]{1,0:T(8,128)(2,1)S(1)}, bf16[64,1536]{1,0:T(8,128)(2,1)S(1)}, u32[]{:S(2)}, u32[]{:S(2)}) collective-permute-start(bf16[64,1536]{1,0:T(8,128)(2,1)S(1)} %shard_map.84.refs_0_), channel_id=1, source_target_pairs={{0,1},{1,0},{2,3},{3,2},{4,5},{5,4},{6,7},{7,6},{8,9},{9,8},{10,11... | collective-permute-start | bytes 589832 | tf_op jit(solution)/shard_map/ppermute | solution.py:240
  35.6 7.2 %collective-permute-start.5 = (bf16[64,1536]{1,0:T(8,128)(2,1)S(1)}, bf16[64,1536]{1,0:T(8,128)(2,1)S(1)}, u32[]{:S(2)}, u32[]{:S(2)}) collective-permute-start(bf16[64,1536]{1,0:T(8,128)(2,1)S(1)} %collective-permute-done.3.refs_1_), channel_id=1, source_target_pairs={{0,1},{1,0},{2,3},{3,2},{4,5},{5,4},{6,7},{7,6},{8,9},{9,8},{10,11... | collective-permute-start | bytes 589832 | tf_op jit(solution)/shard_map/ppermute | solution.py:240
  35.7 19.7 %slice-start = ((s8[4718592]{0:T(1024)(128)(4,1)}), s8[4194304]{0:T(1024)(128)(4,1)S(1)}, s32[]{:S(2)}) async-start(s8[4718592]{0:T(1024)(128)(4,1)} %bitcast.1), calls=%async_computation | async-start | bytes 8388608
  42.8 12.7 %slice-start.1 = ((s8[4718592]{0:T(1024)(128)(4,1)}), s8[524288]{0:T(1024)(128)(4,1)S(1)}, s32[]{:S(2)}) async-start(s8[4718592]{0:T(1024)(128)(4,1)} %bitcast.1), calls=%async_computation.1 | async-start | bytes 1048576

commit v2 on v1

v2 whole, which is shorter than its diff:
```python
import functools
import math

import jax
import jax.numpy as jnp
from jax import lax
from jax.experimental import pallas as pl
from jax.experimental.pallas import tpu as pltpu
from jax.sharding import PartitionSpec as P

H = 12
HD = 128
SCALE = math.log2(math.e) / math.sqrt(HD)
DEAD = -1e30
META_LANES = 512

VMEM = pltpu.VMEM
MEMORY = {"any": jax.ShapeDtypeStruct, "vmem": pltpu.VMEM, "hbm": pltpu.HBM, "scalar": jax.ShapeDtypeStruct}
NT = (((1,), (1,)), ((), ()))


def dot(a, b):
    return jnp.dot(a, b, preferred_element_type=jnp.float32)


def dot_nt(a, b):
    return lax.dot_general(a, b, NT, preferred_element_type=jnp.float32)


def column(row):
    n = row.shape[1]
    shape = (n, n)
    diagonal = lax.broadcasted_iota(jnp.int32, shape, 0) == lax.broadcasted_iota(jnp.int32, shape, 1)
    return jnp.sum(jnp.where(diagonal, jnp.broadcast_to(row, shape), 0.0), axis=1, keepdims=True)


def log_mult(mult):
    return jnp.where(mult > 0.0, jnp.log2(jnp.maximum(mult, 1.0)), DEAD)


def coarse_kernel(
    index_hbm, adjacency_hbm, keys_hbm, values_hbm, coarse_ref, near_ref, keys_ref, values_ref, index_ref, adjacency_ref, sems
):
    load_index = pltpu.make_async_copy(index_hbm, index_ref, sems.at[0])
    load_adjacency = pltpu.make_async_copy(adjacency_hbm, adjacency_ref, sems.at[1])
    load_keys = pltpu.make_async_copy(keys_hbm, keys_ref, sems.at[2])
    load_values = pltpu.make_async_copy(values_hbm, values_ref, sems.at[3])
    for load in (load_index, load_adjacency, load_keys, load_values):
        load.start()
    count = index_ref.shape[1]
    rows = keys_ref.shape[0]
    half = adjacency_ref.shape[2]
    side = 1 - lax.rem(lax.axis_index("band"), 2)
    base = pl.multiple_of(side * half, half)
    load_index.wait()
    picked = column(index_ref[...].astype(jnp.float32))
    slots = lax.broadcasted_iota(jnp.int32, (count, rows), 1).astype(jnp.float32)
    choose = (picked == slots).astype(jnp.bfloat16)
    load_adjacency.wait()
    entries = (adjacency_ref[0, pl.ds(side, 1), :] - base).astype(jnp.float32)
    meta = 2 * (half + count)
    near_ref[meta : meta + 16, 0:half] = jnp.broadcast_to(entries, (16, half)).astype(jnp.bfloat16)
    load_keys.wait()
    coarse = dot(choose, keys_ref[...]).astype(jnp.bfloat16)
    coarse_ref[0:count, :] = coarse
    near_ref[2 * half : 2 * half + count, :] = coarse
    near_ref[0:half, :] = keys_ref[pl.ds(base, half), :]
    load_values.wait()
    coarse = dot(choose, values_ref[...]).astype(jnp.bfloat16)
    coarse_ref[count : 2 * count, :] = coarse
    near_ref[2 * half + count : meta, :] = coarse
    near_ref[half : 2 * half, :] = values_ref[pl.ds(base, half), :]


def multiplicity(entries, live):
    width = entries.shape[1]
    shape = (width, width)
    slot = lax.broadcasted_iota(jnp.int32, shape, 0)
    row = lax.broadcasted_iota(jnp.int32, shape, 1).astype(jnp.float32)
    hits = jnp.where((column(entries) == row) & (slot < live), 1.0, 0.0)
    return jnp.sum(hits, axis=0, keepdims=True)


def boundary_kernel(adjacency_ref, counts_ref, keys_ref, values_ref, far_keys_ref, far_values_ref):
    width = adjacency_ref.shape[2]
    slots = far_keys_ref.shape[0]
    band = lax.axis_index("band")
    odd = lax.rem(band, 2)
    base = pl.multiple_of(odd * width, width)
    entries = (adjacency_ref[0, pl.ds(odd, 1), :] - base).astype(jnp.float32)
    mult = multiplicity(entries, counts_ref[odd, band])
    present = (mult > 0.0).astype(jnp.bfloat16)
    square = (width, width)
    before = lax.broadcasted_iota(jnp.int32, square, 0) < lax.broadcasted_iota(jnp.int32, square, 1)
    order = dot(jnp.broadcast_to(present, (16, width)), before.astype(jnp.bfloat16))[0:1, :]
    place = jnp.where(mult > 0.0, order, -1.0)
    wanted = lax.broadcasted_iota(jnp.int32, (slots, width), 0)
    choose = (wanted.astype(jnp.float32) == place) & (wanted < slots - 1)
    choose = jnp.where(choose, 1.0, 0.0).astype(jnp.bfloat16)
    rows = pl.ds(base, width)
    slot_mult = dot_nt(jnp.broadcast_to(mult.astype(jnp.bfloat16), (16, width)), choose)[0:1, :]
    far_keys_ref[...] = dot(choose, keys_ref[rows, :]).astype(jnp.bfloat16)
    distinct = jnp.sum(jnp.where(mult > 0.0, 1.0, 0.0), axis=1, keepdims=True)
    unused = META_LANES - HD - slots
    meta = jnp.concatenate([slot_mult, jnp.zeros((1, unused), jnp.float32), jnp.broadcast_to(distinct, (1, HD))], axis=1)
    tail = slots - 16
    last = lax.broadcasted_iota(jnp.int32, (16, META_LANES), 0) == 15
    old = far_keys_ref[tail:slots, 0:META_LANES].astype(jnp.float32)
    far_keys_ref[tail:slots, 0:META_LANES] = jnp.where(last, meta, old).astype(jnp.bfloat16)
    far_values_ref[...] = dot(choose, values_ref[rows, :]).astype(jnp.bfloat16)


def head(h):
    return slice(h * HD, (h + 1) * HD)


def with_ones(values):
    return jnp.concatenate([values, jnp.ones_like(values)], axis=1)


def own_kernel(queries_ref, keys_ref, values_ref, high_ref, sums_ref):
    for h in range(H):
        cols = head(h)
        scores = dot_nt(queries_ref[:, cols], keys_ref[:, cols]) * SCALE
        high = jnp.max(scores, axis=1, keepdims=True)
        weights = jnp.exp2(scores - high).astype(jnp.bfloat16)
        sums_ref[h] = dot(weights, with_ones(values_ref[:, cols]))
        high_ref[h] = jnp.broadcast_to(high, high_ref.shape[1:])


def near_kernel(counts_ref, queries_ref, high_in, sums_in, near_ref, *refs):
    high_ref, sums_ref = refs[-2:]
    count = refs[0].shape[0] // 2
    half = (near_ref.shape[0] - 16) // 2 - count
    coarse_refs = refs[:-2] + (near_ref.at[2 * half : 2 * half + 2 * count],)
    band = lax.axis_index("band")
    odd = lax.rem(band, 2)
    meta = 2 * (half + count)
    entries = near_ref[meta : meta + 16, 0:half].astype(jnp.float32)[0:1, :]
    bias = log_mult(multiplicity(entries, counts_ref[odd, band + 1 - 2 * odd]))
    for h in range(H):
        cols = head(h)
        queries = queries_ref[:, cols]
        coarse_keys = jnp.concatenate([ref[0:count, cols] for ref in coarse_refs], axis=0)
        coarse_values = jnp.concatenate([ref[count : 2 * count, cols] for ref in coarse_refs], axis=0)
        scores = [
            dot_nt(queries, near_ref[0:half, cols]) * SCALE + bias,
            dot_nt(queries, coarse_keys) * SCALE,
        ]
        old = high_in[h]
        peaks = [jnp.max(x, axis=1, keepdims=True) for x in scores]
        high = jnp.maximum(old, jnp.maximum(peaks[0], peaks[1]))
        factor = jnp.exp2(old - high)
        weights = [jnp.exp2(x - jnp.concatenate([high] * (x.shape[1] // HD), axis=1)) for x in scores]
        weights = jnp.concatenate([x.astype(jnp.bfloat16) for x in weights], axis=1)
        values = jnp.concatenate([near_ref[half : 2 * half, cols], coarse_values], axis=0)
        sums_ref[h] = sums_in[h] * jnp.concatenate([factor, factor], axis=1) + dot(weights, with_ones(values))
        high_ref[h] = high


def far_kernel(queries_ref, high_ref, sums_ref, sent_keys_ref, far_keys_ref, accum_ref, weights_ref, over_ref):
    slots = far_keys_ref.shape[0]
    padded = weights_ref.shape[2]
    pad = padded - slots
    bands = lax.axis_size("band")
    band = lax.axis_index("band")
    edge = (band == 0) | (band == bands - 1)

    def meta_of(ref):
        meta = ref[slots - 16 : slots, 0:META_LANES].astype(jnp.float32)
        last = lax.broadcasted_iota(jnp.int32, meta.shape, 0) == 15
        return jnp.sum(jnp.where(last, meta, 0.0), axis=0, keepdims=True)

    mult = meta_of(far_keys_ref)
    most = jnp.max(jnp.maximum(mult, meta_of(sent_keys_ref))[:, META_LANES - HD :])
    over_ref[0] = jnp.where((most > slots - 1.0) & jnp.logical_not(edge), 1, 0)
    bias = log_mult(jnp.where(edge, 0.0, mult[:, 0:padded]))
    ones = jnp.ones((padded, HD), jnp.bfloat16)
    for h in range(H):
        cols = head(h)
        keys = jnp.concatenate([far_keys_ref[:, cols], jnp.zeros((pad, HD), jnp.bfloat16)], axis=0)
        scores = dot_nt(queries_ref[:, cols], keys) * SCALE + bias
        old = high_ref[h]
        high = jnp.maximum(old, jnp.max(scores, axis=1, keepdims=True))
        factor = jnp.exp2(old - high)
        weights = jnp.exp2(scores - jnp.concatenate([high] * (padded // HD), axis=1))
        total = sums_ref[h, :, HD:] * factor + dot(weights.astype(jnp.bfloat16), ones)
        inverse = 1.0 / total
        accum_ref[:, cols] = sums_ref[h, :, :HD] * (factor * inverse)
        weights_ref[h] = (weights * jnp.concatenate([inverse] * (padded // HD), axis=1)).astype(jnp.bfloat16)


def project_kernel(accum_ref, weights_ref, far_values_ref, gain_ref, matrix_ref, out_ref, normed_ref):
    rows, width = accum_ref.shape
    chunk = 256
    pad = weights_ref.shape[2] - far_values_ref.shape[0]
    for start in range(0, rows, chunk):
        part = pl.ds(start, chunk)
        heads = [
            accum_ref[part, h * HD : (h + 1) * HD]
            + dot(
                weights_ref[h, part, :],
                jnp.concatenate([far_values_ref[:, head(h)], jnp.zeros((pad, HD), jnp.bfloat16)], axis=0),
            )
            for h in range(H)
        ]
        center = jnp.sum(functools.reduce(jnp.add, heads), axis=1, keepdims=True) * (1.0 / width)
        heads = [x - center for x in heads]
        square = functools.reduce(jnp.add, [x * x for x in heads])
        spread = jnp.sum(square, axis=1, keepdims=True) * (1.0 / width)
        inverse = lax.rsqrt(spread + 1e-05)
        for h, x in enumerate(heads):
            cols = slice(h * HD, (h + 1) * HD)
            normed_ref[part, cols] = (x * inverse * gain_ref[:, cols]).astype(jnp.bfloat16)
        out_ref[part, :] = dot(normed_ref[part, :], matrix_ref[...]).astype(jnp.bfloat16)


def spec(space=VMEM):
    return pl.BlockSpec(memory_space=space)


def call(kernel, ins, outs, scratch=(), limit=24, cost=None):
    flops, nbytes, exps = cost
    ins = [(pltpu.with_memory_space_constraint(x, s) if s is pltpu.HBM else x, s) for x, s in ins]
    return pl.pallas_call(
        kernel,
        in_specs=[spec(s) for _, s in ins],
        out_specs=tuple(spec(pltpu.SMEM if keep == "scalar" else VMEM) for _, _, keep in outs),
        out_shape=tuple(
            MEMORY[keep](shape, dtype) for shape, dtype, keep in outs
        ),
        scratch_shapes=list(scratch),
        compiler_params=pltpu.CompilerParams(vmem_limit_bytes=limit << 20),
        cost_estimate=pl.CostEstimate(flops=flops, bytes_accessed=nbytes, transcendentals=exps),
    )(*[x for x, _ in ins])


def on_device(queries, keys, values, out_gain, out_weight, adjacency, send_counts, coarse_index):
    rows, width = queries.shape
    bands = lax.axis_size("band")
    half = adjacency.shape[2]
    count = coarse_index.shape[0]
    slots = half * 11 // 16
    bf16, f32 = jnp.bfloat16, jnp.float32
    smem = pltpu.SMEM

    def swap(block, mask):
        return lax.ppermute(block, "band", [(i, i ^ mask) for i in range(bands)])

    def far(block):
        slides = lax.axis_size("slide")
        pairs = []
        for slide in range(slides):
            for band in range(bands):
                end = band in (0, bands - 1)
                to = (slide ^ 1, band) if end else (slide, band + 1 if band % 2 else band - 1)
                pairs.append((slide * bands + band, to[0] * bands + to[1]))
        return lax.ppermute(block, ("slide", "band"), pairs)

    def across(block):
        up = [(i, i + 1) for i in range(1, bands - 1, 2)]
        return lax.ppermute(block, "band", up + [(j, i) for i, j in up])

    after = lambda first, x: lax.optimization_barrier((first, x))[1]
    resident = ((rows, width), bf16, "vmem")
    coarse, near, keys, values = call(
        coarse_kernel,
        [(x, pltpu.HBM) for x in (coarse_index.reshape(1, count), adjacency, keys, values)],
        [((2 * count, width), bf16, "any"), ((2 * (half + count) + 16, width), bf16, "any"), resident, resident],
        scratch=[
            pltpu.VMEM((1, count), jnp.int32),
            pltpu.VMEM(adjacency.shape, jnp.int32),
            pltpu.SemaphoreType.DMA((4,)),
        ],
        cost=(4 * count * rows * width, 4 * rows * width, 0),
    )
    mirrored = swap(coarse, bands - 1)
    near = swap(near, 1)
    send_counts = send_counts.T

    def boundary(slots):
        return call(
            boundary_kernel,
            [(adjacency, VMEM), (send_counts, smem), (keys, VMEM), (values, VMEM)],
            [((slots, width), bf16, "any"), ((slots, width), bf16, "any")],
            cost=(1, 1, 0),
        )

    def far_weights(sent_keys, far_keys):
        slots = far_keys.shape[0]
        padded = -(-slots // HD) * HD
        return call(
            far_kernel,
            [(queries, VMEM), (high, VMEM), (sums, VMEM), (sent_keys, VMEM), (far_keys, VMEM)],
            [((rows, width), f32, "vmem"), ((H, rows, padded), bf16, "vmem"), ((1,), jnp.int32, "scalar")],
            cost=(2 * rows * slots * width, 2 * rows * width, H * rows * slots),
        )

    def project(accum, weights, far_values):
        operands = (accum, weights, far_values, out_gain.reshape(1, width), out_weight)
        return call(
            project_kernel,
            [(x, VMEM) for x in operands],
            [((rows, width), bf16, "hbm")],
            scratch=[pltpu.VMEM((rows, width), bf16)],
            cost=(2 * rows * width * (half + width), 2 * width * width, 0),
        )[0]

    sent_keys, sent_values = boundary(slots)
    far_keys, far_values = far(sent_keys), far(sent_values)
    own_keys = after(sent_keys, keys)
    high, sums = call(
        own_kernel,
        [(x, VMEM) for x in [queries, own_keys, values]],
        [((H, rows, HD), f32, "vmem"), ((H, rows, 2 * HD), f32, "vmem")],
        cost=(1, 1, 0),
    )
    mirrored = after(high, mirrored)
    pieces = [coarse, mirrored, swap(mirrored, 1)]
    near_piece = near[2 * half : 2 * (half + count)] if bands > 4 else None
    for mask in [1 << i for i in range(1, bands.bit_length() - 2)]:
        pieces = pieces + [swap(piece, mask) for piece in pieces + [near_piece]]

    state = [((H, rows, HD), f32, "vmem"), ((H, rows, 2 * HD), f32, "vmem")]
    seen = half + bands * count
    high, sums = call(
        near_kernel,
        [(send_counts, smem)] + [(x, VMEM) for x in [queries, high, sums, near] + pieces],
        state,
        cost=(7 * rows * seen * width, 2 * rows * width, H * rows * seen),
    )
    accum, weights, over = far_weights(sent_keys, far_keys)

    def all_rows():
        sent_keys, sent_values = boundary(half + 16)
        far_keys, far_values = across(sent_keys), across(sent_values)
        accum, weights, _ = far_weights(sent_keys, far_keys)
        return project(accum, weights, far_values)

    return lax.cond(over[0] > 0, all_rows, lambda: project(accum, weights, far_values))


def solution(mesh):
    in_specs = (
        P(("slide", "band"), None),
        P(("slide", "band"), None),
        P(("slide", "band"), None),
        P(),
        P(),
        P(("slide", "band"), None, None),
        P("slide", None),
        P(("slide", "band")),
    )
    out_specs = P(("slide", "band"), None)
    return jax.shard_map(
        on_device, mesh=mesh, in_specs=in_specs, out_specs=out_specs, check_vma=False
    )
```

time: 62 us -> 29.4 us (0.47)
  waiting for transfers between devices: 20.3 us -> 1.08 us
  Pallas kernels: 27.8 us -> 21.7 us
  local copies, waits for them, and re-layouts: 4.3 us -> 0.03 us
  starting transfers between devices: 8.91 us -> 5.37 us
    ppermute x6 -> x3, waiting for transfers between devices: 20.3 us -> 1.08 us  [swap(): return lax.ppermute(block, 'band', [(i, i ^ mask) for i in range(bands)])]
    pallas_call x6, Pallas kernels: 27.8 us -> 21.7 us  [call(): pl.pallas_call(kernel, in_specs=[spec(s) for _, s in ins], out_specs=tupl...]
    ppermute x2, starting transfers between devices: 6.46 us -> 1.81 us  [far(): return lax.ppermute(block, ('slide', 'band'), pairs)]
    unnamed x19 -> x12, local copies, waits for them, and re-layouts: 4.3 us -> 0.03 us
    ppermute x6 -> x3, starting transfers between devices: 2.46 us -> 3.56 us  [swap(): return lax.ppermute(block, 'band', [(i, i ^ mask) for i in range(bands)])]
  transfers between devices with their start and end apart: 8 -> 5, of which waited for: 3 -> 1; matrix products, arithmetic and copies ran while one was open for 1% -> 0% of each run, Pallas kernels for 35% -> 48%
where the time goes in v2:
time: 29.4 us; the launch traced here: 28.9 us
  Pallas kernels  21.7 us (74%)
  starting transfers between devices  5.37 us (18%)
  waiting for transfers between devices  1.08 us (4%)
  between operations  0.76 us (3%)
    pallas_call x6, Pallas kernels, call(): pl.pallas_call(kernel, in_specs=[spec(s) for _, s in ins], out_specs=tupl...  21.7 us
    ppermute x3, starting transfers between devices, swap(): return lax.ppermute(block, 'band', [(i, i ^ mask) for i in range(bands)])  3.56 us
    ppermute x2, starting transfers between devices, far(): return lax.ppermute(block, ('slide', 'band'), pairs)  1.81 us
    ppermute x3, waiting for transfers between devices, swap(): return lax.ppermute(block, 'band', [(i, i ^ mask) for i in range(bands)])  1.08 us
  transfers between devices with their start and end apart: 5, of which 1 were waited for; matrix products, arithmetic and copies ran while one was open for 0% of the time, Pallas kernels for 48%

profile of v2, /device:TPU:1, one launch (start us, length us, event | category | flops | bytes accessed | tf_op | source)
XLA Modules:
  0.0 28.9 jit_solution(10164156456875292806)
XLA Ops:
  0.0 0.0 copy-start.2
  0.0 0.0 copy-start.3
  0.0 2.4 %shard_map.84 = (bf16[64,1536]{1,0:T(8,128)(2,1)S(1)}, bf16[592,1536]{1,0:T(8,128)(2,1)S(1)}, bf16[512,1536]{1,0:T(8,128)(2,1)S(1)}, bf16[512,1536]{1,0:T(8,128)(2,1)S(1)}) custom-call(s32[1,32]{1,0:T(1,128)} %bitcast.8, s32[1,2,256]{2,1,0:T(2,128)} %adjacency_ref.1, bf16[512,1536]{1,0:T(8,128)(2,1)} %keys_hbm.1, bf16[512,1536]{1,0:T(8,128)(2,1)} %values_hbm.1), custom_call_target="tpu_custom_call" | custom-call | flops 100663296 | bytes 3145728 | tf_op jit(solution)/shard_map/pallas_call | solution.py:225
  2.4 0.0 copy-start
  2.4 0.1 collective-permute-start.2
  2.6 2.7 %collective-permute-start.3 = (bf16[64,1536]{1,0:T(8,128)(2,1)S(1)}, bf16[64,1536]{1,0:T(8,128)(2,1)S(1)}, u32[]{:S(2)}, u32[]{:S(2)}) collective-permute-start(bf16[64,1536]{1,0:T(8,128)(2,1)S(1)} %get-tuple-element.76.refs_0_), channel_id=1, source_target_pairs={{0,3},{1,2},{2,1},{3,0},{4,7},{5,6},{6,5},{7,4},{8,11},{9,10},{10,... | collective-permute-start | bytes 589832 | tf_op jit(solution)/shard_map/ppermute | solution.py:248
  5.2 0.0 copy-done.2
  5.2 0.0 copy-done.3
  5.2 1.3 %shard_map.85 = (bf16[176,1536]{1,0:T(8,128)(2,1)S(1)}, bf16[176,1536]{1,0:T(8,128)(2,1)S(1)}) custom-call(s32[1,2,256]{2,1,0:T(2,128)S(1)} %copy-done.2, s32[2,4]{1,0:T(2,128)S(1)} %bitcast.5, bf16[512,1536]{1,0:T(8,128)(2,1)S(1)} %get-tuple-element.72.keys_ref, bf16[512,1536]{1,0:T(8,128)(2,1)S(1)} %get-tuple-element.70.values_ref), custom_call_target="tpu_custom_call" | custom-call | flops 1 | bytes 1 | tf_op jit(solution)/shard_map/pallas_call | solution.py:225
  6.5 0.1 collective-permute-start.5
  6.6 1.7 %collective-permute-start.6 = (bf16[176,1536]{1,0:T(8,128)(2,1)S(1)}, bf16[176,1536]{1,0:T(8,128)(2,1)S(1)}, u32[]{:S(2)}, u32[]{:S(2)}) collective-permute-start(bf16[176,1536]{1,0:T(8,128)(2,1)S(1)} %get-tuple-element.83), channel_id=1, source_target_pairs={{0,4},{1,2},{2,1},{3,7},{4,0},{5,6},{6,5},{7,3},{8,12},{9,10},{10,... | collective-permute-start | bytes 1622024 | tf_op jit(solution)/shard_map/ppermute | solution.py:258
  8.3 0.0 copy-done
  8.3 0.0 slice-start
  8.3 3.9 %shard_map.86 = (f32[12,512,128]{2,1,0:T(8,128)S(1)}, f32[12,512,256]{2,1,0:T(8,128)S(1)}) custom-call(bf16[512,1536]{1,0:T(8,128)(2,1)S(1)} %copy-done, bf16[512,1536]{1,0:T(8,128)(2,1)S(1)} %get-tuple-element.72.keys_ref, bf16[512,1536]{1,0:T(8,128)(2,1)S(1)} %get-tuple-element.70.values_ref), custom_call_target="tpu_custom_call" | custom-call | flops 1 | bytes 1 | tf_op jit(solution)/shard_map/pallas_call | solution.py:225
  12.2 0.0 collective-permute-done.3.refs_1_
  12.2 0.8 %collective-permute-start.4 = (bf16[64,1536]{1,0:T(8,128)(2,1)S(1)}, bf16[64,1536]{1,0:T(8,128)(2,1)S(1)}, u32[]{:S(2)}, u32[]{:S(2)}) collective-permute-start(bf16[64,1536]{1,0:T(8,128)(2,1)S(1)} %collective-permute-done.3.refs_1_), channel_id=1, source_target_pairs={{0,1},{1,0},{2,3},{3,2},{4,5},{5,4},{6,7},{7,6},{8,9},{9,8},{10,11... | collective-permute-start | bytes 589832 | tf_op jit(solution)/shard_map/ppermute | solution.py:248
  13.0 1.1 %collective-permute-done.4.refs_2_ = bf16[64,1536]{1,0:T(8,128)(2,1)S(1)} collective-permute-done((bf16[64,1536]{1,0:T(8,128)(2,1)S(1)}, bf16[64,1536]{1,0:T(8,128)(2,1)S(1)}, u32[]{:S(2)}, u32[]{:S(2)}) %collective-permute-start.4) | collective-permute-done | bytes 196640 | tf_op jit(solution)/shard_map/ppermute | solution.py:248
  14.0 0.0 collective-permute-done.2.near_ref
  14.0 0.0 slice-start.1
  14.1 5.1 %shard_map.87 = (f32[12,512,128]{2,1,0:T(8,128)S(1)}, f32[12,512,256]{2,1,0:T(8,128)S(1)}) custom-call(s32[2,4]{1,0:T(2,128)S(1)} %bitcast.6, bf16[512,1536]{1,0:T(8,128)(2,1)S(1)} %copy-done, f32[12,512,128]{2,1,0:T(8,128)S(1)} %get-tuple-element.73.high_in, f32[12,512,256]{2,1,0:T(8,128)S(1)} %get-tuple-element.74.sums_in, ...), custom_call_target="tpu_custom_call" | custom-call | flops 2113929216 | bytes 1572864 | tf_op jit(solution)/shard_map/pallas_call | solution.py:225
  19.2 0.0 collective-permute-done.5.far_keys_ref
  19.2 0.0 copy-start.1
  19.2 3.5 %shard_map.88 = (f32[512,1536]{1,0:T(8,128)S(1)}, bf16[12,512,256]{2,1,0:T(8,128)(2,1)S(1)}, s32[1]{0:T(128)}) custom-call(bf16[512,1536]{1,0:T(8,128)(2,1)S(1)} %copy-done, f32[12,512,128]{2,1,0:T(8,128)S(1)} %get-tuple-element.78.high_ref, f32[12,512,256]{2,1,0:T(8,128)S(1)} %get-tuple-element.79.sums_ref, ...), custom_call_target="tpu_custom_call" | custom-call | flops 276824064 | bytes 1572864 | tf_op jit(solution)/shard_map/pallas_call | solution.py:225
  23.3 0.0 collective-permute-done.6
  23.4 0.0 slice-done
  23.4 0.0 slice-done.1
  23.4 0.0 copy-done.1
  23.4 5.5 %conditional.1 = (bf16[512,1536]{1,0:T(8,128)(2,1)}) conditional(s32[]{:T(128)} %bitcast.2, (f32[1536]{0:T(1024)S(1)}, f32[512,1536]{1,0:T(8,128)S(1)}, bf16[12,512,256]{2,1,0:T(8,128)(2,1)S(1)}, bf16[176,1536]{1,0:T(8,128)(2,1)S(1)}, bf16[1536,1536]{1,0:T(8,128)(2,1)S(1)}) %tuple.24, (s32[1,2,256]{2,1,0:T(2,128)S(1)}, s32[2,4]{1,0:T(2,128)S(1)}, ...), branch_computations={%region_0.0_spmd, %region_1.0_spmd} | conditional | flops 3246391296 | bytes 12988505 | solution.py:340
  23.4 5.5 %branch_0_fun.1 = bf16[512,1536]{1,0:T(8,128)(2,1)} custom-call(f32[512,1536]{1,0:T(8,128)S(1)} %get-tuple-element.36.accum_ref, bf16[12,512,256]{2,1,0:T(8,128)(2,1)S(1)} %get-tuple-element.37.weights_ref, bf16[176,1536]{1,0:T(8,128)(2,1)S(1)} %get-tuple-element.38.far_values_ref, f32[1,1536]{1,0:T(1,128)S(1)} %reshape.10.gain_ref, ...), custom_call_target="tpu_custom_call" | custom-call | flops 2818572288 | bytes 4718592 | tf_op jit(solution)/shard_map/cond/branch_0_fun/pallas_call | solution.py:225
  (2 shorter events, 0.0 us)
Async XLA Ops:
  0.0 5.2 %copy-start.2 = (s32[1,2,256]{2,1,0:T(2,128)S(1)}, s32[1,2,256]{2,1,0:T(2,128)}, u32[]{:S(2)}) copy-start(s32[1,2,256]{2,1,0:T(2,128)} %adjacency_ref.1) | copy-start | bytes 6148
  0.0 5.2 %copy-start.3 = (s32[4,2]{0,1:T(2,128)S(1)}, s32[4,2]{0,1:T(2,128)}, u32[]{:S(2)}) copy-start(s32[4,2]{0,1:T(2,128)} %param.16) | copy-start | bytes 100
  2.4 5.9 %copy-start = (bf16[512,1536]{1,0:T(8,128)(2,1)S(1)}, bf16[512,1536]{1,0:T(8,128)(2,1)}, u32[]{:S(2)}) copy-start(bf16[512,1536]{1,0:T(8,128)(2,1)} %queries_ref.5) | copy-start | bytes 4718596
  2.4 11.6 %collective-permute-start.2 = (bf16[592,1536]{1,0:T(8,128)(2,1)S(1)}, bf16[592,1536]{1,0:T(8,128)(2,1)S(1)}, u32[]{:S(2)}, u32[]{:S(2)}) collective-permute-start(bf16[592,1536]{1,0:T(8,128)(2,1)S(1)} %get-tuple-element.75), channel_id=1, source_target_pairs={{0,1},{1,0},{2,3},{3,2},{4,5},{5,4},{6,7},{7,6},{8,9},{9,8},{10,11... | collective-permute-start | bytes 5455880 | tf_op jit(solution)/shard_map/ppermute | solution.py:248
  2.6 9.6 %collective-permute-start.3 = (bf16[64,1536]{1,0:T(8,128)(2,1)S(1)}, bf16[64,1536]{1,0:T(8,128)(2,1)S(1)}, u32[]{:S(2)}, u32[]{:S(2)}) collective-permute-start(bf16[64,1536]{1,0:T(8,128)(2,1)S(1)} %get-tuple-element.76.refs_0_), channel_id=1, source_target_pairs={{0,3},{1,2},{2,1},{3,0},{4,7},{5,6},{6,5},{7,4},{8,11},{9,10},{10,... | collective-permute-start | bytes 589832 | tf_op jit(solution)/shard_map/ppermute | solution.py:248
  6.5 12.7 %collective-permute-start.5 = (bf16[176,1536]{1,0:T(8,128)(2,1)S(1)}, bf16[176,1536]{1,0:T(8,128)(2,1)S(1)}, u32[]{:S(2)}, u32[]{:S(2)}) collective-permute-start(bf16[176,1536]{1,0:T(8,128)(2,1)S(1)} %get-tuple-element.71.sent_keys_ref), channel_id=1, source_target_pairs={{0,4},{1,2},{2,1},{3,7},{4,0},{5,6},{6,5},{7,3},{8,12},{9,10},{10,... | collective-permute-start | bytes 1622024 | tf_op jit(solution)/shard_map/ppermute | solution.py:258
  6.6 16.8 %collective-permute-start.6 = (bf16[176,1536]{1,0:T(8,128)(2,1)S(1)}, bf16[176,1536]{1,0:T(8,128)(2,1)S(1)}, u32[]{:S(2)}, u32[]{:S(2)}) collective-permute-start(bf16[176,1536]{1,0:T(8,128)(2,1)S(1)} %get-tuple-element.83), channel_id=1, source_target_pairs={{0,4},{1,2},{2,1},{3,7},{4,0},{5,6},{6,5},{7,3},{8,12},{9,10},{10,... | collective-permute-start | bytes 1622024 | tf_op jit(solution)/shard_map/ppermute | solution.py:258
  8.3 15.1 %slice-start = ((s8[4718592]{0:T(1024)(128)(4,1)}), s8[4194304]{0:T(1024)(128)(4,1)S(1)}, s32[]{:S(2)}) async-start(s8[4718592]{0:T(1024)(128)(4,1)} %bitcast.3), calls=%async_computation | async-start | bytes 8388608
  12.2 1.9 %collective-permute-start.4 = (bf16[64,1536]{1,0:T(8,128)(2,1)S(1)}, bf16[64,1536]{1,0:T(8,128)(2,1)S(1)}, u32[]{:S(2)}, u32[]{:S(2)}) collective-permute-start(bf16[64,1536]{1,0:T(8,128)(2,1)S(1)} %collective-permute-done.3.refs_1_), channel_id=1, source_target_pairs={{0,1},{1,0},{2,3},{3,2},{4,5},{5,4},{6,7},{7,6},{8,9},{9,8},{10,11... | collective-permute-start | bytes 589832 | tf_op jit(solution)/shard_map/ppermute | solution.py:248
  14.0 9.3 %slice-start.1 = ((s8[4718592]{0:T(1024)(128)(4,1)}), s8[524288]{0:T(1024)(128)(4,1)S(1)}, s32[]{:S(2)}) async-start(s8[4718592]{0:T(1024)(128)(4,1)} %bitcast.3), calls=%async_computation.1 | async-start | bytes 1048576
  19.2 4.2 %copy-start.1 = (f32[1536]{0:T(1024)S(1)}, f32[1536]{0:T(1024)}, u32[]{:S(2)}) copy-start(f32[1536]{0:T(1024)} %param.13) | copy-start | bytes 18436

commit v3 on v2

--- a/solution.py
+++ b/solution.py
@@ -12,10 +12,13 @@
 HD = 128
 SCALE = math.log2(math.e) / math.sqrt(HD)
 DEAD = -1e30
+BLOCKS = 3
+GROUPS = 2
 META_LANES = 512
 
 VMEM = pltpu.VMEM
 MEMORY = {"any": jax.ShapeDtypeStruct, "vmem": pltpu.VMEM, "hbm": pltpu.HBM, "scalar": jax.ShapeDtypeStruct}
+SPACE = {"scalar": pltpu.SMEM, "hbm": pltpu.HBM}
 NT = (((1,), (1,)), ((), ()))
 
 
@@ -114,51 +117,45 @@
     return slice(h * HD, (h + 1) * HD)
 
 
+def tiles(x):
+    return [x[:, i : i + HD] for i in range(0, x.shape[1], HD)]
+
+
+def across_tiles(slab, columns):
+    return jnp.concatenate([slab] * (columns // HD), axis=1)
+
+
 def with_ones(values):
     return jnp.concatenate([values, jnp.ones_like(values)], axis=1)
 
 
-def own_kernel(queries_ref, keys_ref, values_ref, high_ref, sums_ref):
-    for h in range(H):
-        cols = head(h)
-        scores = dot_nt(queries_ref[:, cols], keys_ref[:, cols]) * SCALE
-        high = jnp.max(scores, axis=1, keepdims=True)
-        weights = jnp.exp2(scores - high).astype(jnp.bfloat16)
-        sums_ref[h] = dot(weights, with_ones(values_ref[:, cols]))
-        high_ref[h] = jnp.broadcast_to(high, high_ref.shape[1:])
-
-
-def near_kernel(counts_ref, queries_ref, high_in, sums_in, near_ref, *refs):
-    high_ref, sums_ref = refs[-2:]
-    count = refs[0].shape[0] // 2
-    half = (near_ref.shape[0] - 16) // 2 - count
-    coarse_refs = refs[:-2] + (near_ref.at[2 * half : 2 * half + 2 * count],)
+def near_kernel(half, first, counts_ref, queries_ref, keys_ref, values_ref, near_ref, high_ref, sums_ref):
     band = lax.axis_index("band")
     odd = lax.rem(band, 2)
-    meta = 2 * (half + count)
-    entries = near_ref[meta : meta + 16, 0:half].astype(jnp.float32)[0:1, :]
+    entries = near_ref[near_ref.shape[0] - 16 :, 0:half].astype(jnp.float32)[0:1, :]
     bias = log_mult(multiplicity(entries, counts_ref[odd, band + 1 - 2 * odd]))
-    for h in range(H):
-        cols = head(h)
+    for h in range(high_ref.shape[0]):
+        cols = head(first + h)
         queries = queries_ref[:, cols]
-        coarse_keys = jnp.concatenate([ref[0:count, cols] for ref in coarse_refs], axis=0)
-        coarse_values = jnp.concatenate([ref[count : 2 * count, cols] for ref in coarse_refs], axis=0)
         scores = [
+            dot_nt(queries, keys_ref[:, cols]) * SCALE,
             dot_nt(queries, near_ref[0:half, cols]) * SCALE + bias,
-            dot_nt(queries, coarse_keys) * SCALE,
         ]
-        old = high_in[h]
-        peaks = [jnp.max(x, axis=1, keepdims=True) for x in scores]
-        high = jnp.maximum(old, jnp.maximum(peaks[0], peaks[1]))
-        factor = jnp.exp2(old - high)
-        weights = [jnp.exp2(x - jnp.concatenate([high] * (x.shape[1] // HD), axis=1)) for x in scores]
-        weights = jnp.concatenate([x.astype(jnp.bfloat16) for x in weights], axis=1)
-        values = jnp.concatenate([near_ref[half : 2 * half, cols], coarse_values], axis=0)
-        sums_ref[h] = sums_in[h] * jnp.concatenate([factor, factor], axis=1) + dot(weights, with_ones(values))
-        high_ref[h] = high
-
-
-def far_kernel(queries_ref, high_ref, sums_ref, sent_keys_ref, far_keys_ref, accum_ref, weights_ref, over_ref):
+        high = jnp.maximum(*[jnp.max(x, axis=1, keepdims=True) for x in scores])
+        weights = jnp.concatenate([jnp.exp2(x - high).astype(jnp.bfloat16) for x in scores], axis=1)
+        values = jnp.concatenate([values_ref[:, cols], near_ref[half : 2 * half, cols]], axis=0)
+        sums_ref[h] = dot(weights, with_ones(values))
+        high_ref[h] = jnp.broadcast_to(high, high_ref.shape[1:])
+
+
+def far_kernel(exact, groups, queries_ref, sent_keys_ref, far_keys_ref, near_ref, *refs):
+    states, (accum_ref, weights_ref, state_ref) = refs[: 2 * groups], refs[-3:]
+    coarse_refs = refs[2 * groups : -3]
+    coarse = coarse_refs[0].shape[0]
+    count = coarse // 2
+    end = near_ref.shape[0] - 16
+    coarse_refs += (near_ref.at[end - coarse : end],)
+    rows = queries_ref.shape[0]
     slots = far_keys_ref.shape[0]
     padded = weights_ref.shape[2]
     pad = padded - slots
@@ -173,31 +170,45 @@
 
     mult = meta_of(far_keys_ref)
     most = jnp.max(jnp.maximum(mult, meta_of(sent_keys_ref))[:, META_LANES - HD :])
-    over_ref[0] = jnp.where((most > slots - 1.0) & jnp.logical_not(edge), 1, 0)
+    overflow = (most > slots - 1.0) & jnp.logical_not(edge)
     bias = log_mult(jnp.where(edge, 0.0, mult[:, 0:padded]))
     ones = jnp.ones((padded, HD), jnp.bfloat16)
+    all_totals = jnp.zeros((rows, HD), jnp.float32)
     for h in range(H):
+        high_ref, sums_ref = states[2 * (h * groups // H) : 2 * (h * groups // H) + 2]
+        place = h % (H // groups)
         cols = head(h)
+        queries = queries_ref[:, cols]
         keys = jnp.concatenate([far_keys_ref[:, cols], jnp.zeros((pad, HD), jnp.bfloat16)], axis=0)
-        scores = dot_nt(queries_ref[:, cols], keys) * SCALE + bias
-        old = high_ref[h]
-        high = jnp.maximum(old, jnp.max(scores, axis=1, keepdims=True))
-        factor = jnp.exp2(old - high)
-        weights = jnp.exp2(scores - jnp.concatenate([high] * (padded // HD), axis=1))
-        total = sums_ref[h, :, HD:] * factor + dot(weights.astype(jnp.bfloat16), ones)
+        coarse_keys = jnp.concatenate([ref[0:count, cols] for ref in coarse_refs], axis=0)
+        coarse_values = jnp.concatenate([ref[count:coarse, cols] for ref in coarse_refs], axis=0)
+        scores = dot_nt(queries, keys) * SCALE + bias
+        coarse_scores = dot_nt(queries, coarse_keys) * SCALE
+        high, summed = high_ref[place], sums_ref[place]
+        if exact:
+            peak = functools.reduce(jnp.maximum, tiles(scores) + tiles(coarse_scores))
+            old, high = high, jnp.maximum(high, jnp.max(peak, axis=1, keepdims=True))
+            summed = summed * across_tiles(jnp.exp2(old - high), 2 * HD)
+        weights = jnp.exp2(scores - across_tiles(high, padded))
+        coarse_weights = jnp.exp2(coarse_scores - across_tiles(high, coarse_scores.shape[1])).astype(jnp.bfloat16)
+        summed = summed + dot(coarse_weights, with_ones(coarse_values))
+        total = summed[:, HD:] + dot(weights.astype(jnp.bfloat16), ones)
+        all_totals = all_totals + total
         inverse = 1.0 / total
-        accum_ref[:, cols] = sums_ref[h, :, :HD] * (factor * inverse)
-        weights_ref[h] = (weights * jnp.concatenate([inverse] * (padded // HD), axis=1)).astype(jnp.bfloat16)
-
-
-def project_kernel(accum_ref, weights_ref, far_values_ref, gain_ref, matrix_ref, out_ref, normed_ref):
+        accum_ref[:, cols] = summed[:, :HD] * inverse
+        weights_ref[h] = (weights * across_tiles(inverse, padded)).astype(jnp.bfloat16)
+    safe = jnp.max(all_totals) < 2.0**100
+    state_ref[0] = jnp.where(overflow, 2, jnp.where(safe | exact, 0, 1))
+
+
+def project_kernel(accum_ref, weights_ref, far_values_ref, gain_ref, matrix_ref, out_hbm, normed_ref, out_ref, sems):
     rows, width = accum_ref.shape
+    pad = weights_ref.shape[2] - far_values_ref.shape[0]
     chunk = 256
-    pad = weights_ref.shape[2] - far_values_ref.shape[0]
     for start in range(0, rows, chunk):
         part = pl.ds(start, chunk)
         heads = [
-            accum_ref[part, h * HD : (h + 1) * HD]
+            accum_ref[part, head(h)]
             + dot(
                 weights_ref[h, part, :],
                 jnp.concatenate([far_values_ref[:, head(h)], jnp.zeros((pad, HD), jnp.bfloat16)], axis=0),
@@ -210,9 +221,16 @@
         spread = jnp.sum(square, axis=1, keepdims=True) * (1.0 / width)
         inverse = lax.rsqrt(spread + 1e-05)
         for h, x in enumerate(heads):
-            cols = slice(h * HD, (h + 1) * HD)
-            normed_ref[part, cols] = (x * inverse * gain_ref[:, cols]).astype(jnp.bfloat16)
-        out_ref[part, :] = dot(normed_ref[part, :], matrix_ref[...]).astype(jnp.bfloat16)
+            normed_ref[part, head(h)] = (x * inverse * gain_ref[:, head(h)]).astype(jnp.bfloat16)
+    block = width // BLOCKS
+    copies = []
+    for i in range(BLOCKS):
+        cols = pl.ds(i * block, block)
+        out_ref[:, cols] = dot(normed_ref[...], matrix_ref[:, cols]).astype(jnp.bfloat16)
+        copies.append(pltpu.make_async_copy(out_ref.at[:, cols], out_hbm.at[:, cols], sems.at[i]))
+        copies[-1].start()
+    for copy in copies:
+        copy.wait()
 
 
 def spec(space=VMEM):
@@ -225,7 +243,7 @@
     return pl.pallas_call(
         kernel,
         in_specs=[spec(s) for _, s in ins],
-        out_specs=tuple(spec(pltpu.SMEM if keep == "scalar" else VMEM) for _, _, keep in outs),
+        out_specs=tuple(spec(SPACE.get(keep, VMEM)) for _, _, keep in outs),
         out_shape=tuple(
             MEMORY[keep](shape, dtype) for shape, dtype, keep in outs
         ),
@@ -286,58 +304,61 @@
             cost=(1, 1, 0),
         )
 
-    def far_weights(sent_keys, far_keys):
+    def far_weights(exact, states, sent_keys, far_keys):
         slots = far_keys.shape[0]
         padded = -(-slots // HD) * HD
         return call(
-            far_kernel,
-            [(queries, VMEM), (high, VMEM), (sums, VMEM), (sent_keys, VMEM), (far_keys, VMEM)],
+            functools.partial(far_kernel, exact, len(states)),
+            [(x, VMEM) for x in [queries, sent_keys, far_keys, near] + sum(states, []) + pieces],
             [((rows, width), f32, "vmem"), ((H, rows, padded), bf16, "vmem"), ((1,), jnp.int32, "scalar")],
-            cost=(2 * rows * slots * width, 2 * rows * width, H * rows * slots),
+            cost=(4 * rows * slots * width, 2 * rows * width, H * rows * slots),
         )
 
     def project(accum, weights, far_values):
-        operands = (accum, weights, far_values, out_gain.reshape(1, width), out_weight)
+        operands = (accum, weights, far_values, gain, out_weight)
         return call(
             project_kernel,
             [(x, VMEM) for x in operands],
             [((rows, width), bf16, "hbm")],
-            scratch=[pltpu.VMEM((rows, width), bf16)],
+            scratch=[pltpu.VMEM((rows, width), bf16)] * 2 + [pltpu.SemaphoreType.DMA((BLOCKS,))],
             cost=(2 * rows * width * (half + width), 2 * width * width, 0),
         )[0]
 
     sent_keys, sent_values = boundary(slots)
-    far_keys, far_values = far(sent_keys), far(sent_values)
+    far_values = far(sent_values)
+    far_keys = far(sent_keys)
     own_keys = after(sent_keys, keys)
-    high, sums = call(
-        own_kernel,
-        [(x, VMEM) for x in [queries, own_keys, values]],
-        [((H, rows, HD), f32, "vmem"), ((H, rows, 2 * HD), f32, "vmem")],
-        cost=(1, 1, 0),
-    )
-    mirrored = after(high, mirrored)
+    states = []
+    for group in range(GROUPS):
+        heads = H // GROUPS
+        high, sums = call(
+            functools.partial(near_kernel, half, group * heads),
+            [(send_counts, smem)] + [(x, VMEM) for x in [queries, own_keys, values, near]],
+            [((heads, rows, HD), f32, "vmem"), ((heads, rows, 2 * HD), f32, "vmem")],
+            cost=(22 * group * rows * half * width, 2, 0),
+        )
+        states.append([high, sums])
+        if group == 0:
+            mirrored = after(high, mirrored)
+            own_keys = after(mirrored, own_keys)
     pieces = [coarse, mirrored, swap(mirrored, 1)]
     near_piece = near[2 * half : 2 * (half + count)] if bands > 4 else None
     for mask in [1 << i for i in range(1, bands.bit_length() - 2)]:
         pieces = pieces + [swap(piece, mask) for piece in pieces + [near_piece]]
-
-    state = [((H, rows, HD), f32, "vmem"), ((H, rows, 2 * HD), f32, "vmem")]
-    seen = half + bands * count
-    high, sums = call(
-        near_kernel,
-        [(send_counts, smem)] + [(x, VMEM) for x in [queries, high, sums, near] + pieces],
-        state,
-        cost=(7 * rows * seen * width, 2 * rows * width, H * rows * seen),
-    )
-    accum, weights, over = far_weights(sent_keys, far_keys)
+    accum, weights, state = far_weights(False, states, sent_keys, far_keys)
+    gain = after(accum, out_gain.reshape(1, width))
+
+    def exact():
+        accum, weights, _ = far_weights(True, states, sent_keys, far_keys)
+        return project(accum, weights, far_values)
 
     def all_rows():
         sent_keys, sent_values = boundary(half + 16)
         far_keys, far_values = across(sent_keys), across(sent_values)
-        accum, weights, _ = far_weights(sent_keys, far_keys)
+        accum, weights, _ = far_weights(True, states, sent_keys, far_keys)
         return project(accum, weights, far_values)
 
-    return lax.cond(over[0] > 0, all_rows, lambda: project(accum, weights, far_values))
+    return lax.switch(state[0], [lambda: project(accum, weights, far_values), exact, all_rows])
 
 
 def solution(mesh):

time: 29.4 us -> 32.9 us (1.12); the launches traced: 28.9 us -> 32.8 us
  Pallas kernels: 21.7 us -> 26.2 us
  waiting for transfers between devices: 1.08 us -> 0.01 us
    pallas_call x6 -> x7, Pallas kernels: 21.7 us -> 26.2 us  [call(): pl.pallas_call(kernel, in_specs=[spec(s) for _, s in ins], out_specs=tupl...]
    ppermute x3, waiting for transfers between devices: 1.08 us -> 0.01 us  [swap(): return lax.ppermute(block, 'band', [(i, i ^ mask) for i in range(bands)])]
  transfers between devices with their start and end apart: 5 -> 5, of which waited for: 1 -> 0; matrix products, arithmetic and copies ran while one was open for 0% -> 0% of each run, Pallas kernels for 48% -> 41%
where the time goes in v3:
time: 32.9 us; the launch traced here: 32.8 us
  Pallas kernels  26.2 us (80%)
  starting transfers between devices  5.37 us (16%)
  between operations  0.95 us (3%)
    pallas_call x7, Pallas kernels, call(): pl.pallas_call(kernel, in_specs=[spec(s) for _, s in ins], out_specs=tupl...  26.2 us
    ppermute x3, starting transfers between devices, swap(): return lax.ppermute(block, 'band', [(i, i ^ mask) for i in range(bands)])  3.56 us
    ppermute x2, starting transfers between devices, far(): return lax.ppermute(block, ('slide', 'band'), pairs)  1.81 us
  transfers between devices with their start and end apart: 5, of which 0 were waited for; matrix products, arithmetic and copies ran while one was open for 0% of the time, Pallas kernels for 41%

profile of v3, /device:TPU:1, one launch (start us, length us, event | category | flops | bytes accessed | tf_op | source)
XLA Modules:
  0.0 32.8 jit_solution(15722365485704367223)
XLA Ops:
  0.0 0.0 copy-start.1
  0.0 0.0 copy-start.2
  0.0 2.4 %shard_map.85 = (bf16[64,1536]{1,0:T(8,128)(2,1)S(1)}, bf16[592,1536]{1,0:T(8,128)(2,1)S(1)}, bf16[512,1536]{1,0:T(8,128)(2,1)S(1)}, bf16[512,1536]{1,0:T(8,128)(2,1)S(1)}) custom-call(s32[1,32]{1,0:T(1,128)} %bitcast.9, s32[1,2,256]{2,1,0:T(2,128)} %adjacency_ref.1, bf16[512,1536]{1,0:T(8,128)(2,1)} %keys_hbm.1, bf16[512,1536]{1,0:T(8,128)(2,1)} %values_hbm.1), custom_call_target="tpu_custom_call" | custom-call | flops 100663296 | bytes 3145728 | tf_op jit(solution)/shard_map/pallas_call | solution.py:243
  2.4 0.0 copy-start.3
  2.4 0.0 copy-start
  2.4 0.1 collective-permute-start.3
  2.6 2.7 %collective-permute-start.4 = (bf16[64,1536]{1,0:T(8,128)(2,1)S(1)}, bf16[64,1536]{1,0:T(8,128)(2,1)S(1)}, u32[]{:S(2)}, u32[]{:S(2)}) collective-permute-start(bf16[64,1536]{1,0:T(8,128)(2,1)S(1)} %get-tuple-element.141.refs_4_), channel_id=1, source_target_pairs={{0,3},{1,2},{2,1},{3,0},{4,7},{5,6},{6,5},{7,4},{8,11},{9,10},{10,... | collective-permute-start | bytes 589832 | tf_op jit(solution)/shard_map/ppermute | solution.py:266
  5.2 0.0 copy-done.1
  5.2 0.0 copy-done.2
  5.2 1.3 %shard_map.86 = (bf16[176,1536]{1,0:T(8,128)(2,1)S(1)}, bf16[176,1536]{1,0:T(8,128)(2,1)S(1)}) custom-call(s32[1,2,256]{2,1,0:T(2,128)S(1)} %copy-done.1, s32[2,4]{1,0:T(2,128)S(1)} %bitcast.5, bf16[512,1536]{1,0:T(8,128)(2,1)S(1)} %get-tuple-element.143.keys_ref, bf16[512,1536]{1,0:T(8,128)(2,1)S(1)} %get-tuple-element.135.values_ref), custom_call_target="tpu_custom_call" | custom-call | flops 1 | bytes 1 | tf_op jit(solution)/shard_map/pallas_call | solution.py:243
  6.5 0.1 collective-permute-start.2
  6.6 1.7 %collective-permute-start.6 = (bf16[176,1536]{1,0:T(8,128)(2,1)S(1)}, bf16[176,1536]{1,0:T(8,128)(2,1)S(1)}, u32[]{:S(2)}, u32[]{:S(2)}) collective-permute-start(bf16[176,1536]{1,0:T(8,128)(2,1)S(1)} %get-tuple-element.149), channel_id=1, source_target_pairs={{0,4},{1,2},{2,1},{3,7},{4,0},{5,6},{6,5},{7,3},{8,12},{9,10},{10,... | collective-permute-start | bytes 1622024 | tf_op jit(solution)/shard_map/ppermute | solution.py:276
  8.3 0.0 copy-done.3
  8.3 0.0 collective-permute-done.3.near_ref
  8.3 0.0 copy-done
  8.3 0.0 slice-start
  8.4 4.0 %shard_map.87 = (f32[6,512,128]{2,1,0:T(8,128)S(1)}, f32[6,512,256]{2,1,0:T(8,128)S(1)}) custom-call(s32[2,4]{1,0:T(2,128)S(1)} %bitcast.6, bf16[512,1536]{1,0:T(8,128)(2,1)S(1)} %copy-done, bf16[512,1536]{1,0:T(8,128)(2,1)S(1)} %get-tuple-element.143.keys_ref, bf16[512,1536]{1,0:T(8,128)(2,1)S(1)} %get-tuple-element.135.values_ref, ...), custom_call_target="tpu_custom_call" | custom-call | bytes 2 | tf_op jit(solution)/shard_map/pallas_call | solution.py:243
  12.3 0.0 collective-permute-done.4.refs_5_
  12.3 0.0 slice-start.1
  12.4 0.8 %collective-permute-start.5 = (bf16[64,1536]{1,0:T(8,128)(2,1)S(1)}, bf16[64,1536]{1,0:T(8,128)(2,1)S(1)}, u32[]{:S(2)}, u32[]{:S(2)}) collective-permute-start(bf16[64,1536]{1,0:T(8,128)(2,1)S(1)} %collective-permute-done.4.refs_5_), channel_id=1, source_target_pairs={{0,1},{1,0},{2,3},{3,2},{4,5},{5,4},{6,7},{7,6},{8,9},{9,8},{10,11... | collective-permute-start | bytes 589832 | tf_op jit(solution)/shard_map/ppermute | solution.py:266
  13.1 4.0 %shard_map.88 = (f32[6,512,128]{2,1,0:T(8,128)S(1)}, f32[6,512,256]{2,1,0:T(8,128)S(1)}) custom-call(s32[2,4]{1,0:T(2,128)S(1)} %bitcast.7, bf16[512,1536]{1,0:T(8,128)(2,1)S(1)} %copy-done, bf16[512,1536]{1,0:T(8,128)(2,1)S(1)} %get-tuple-element.143.keys_ref, bf16[512,1536]{1,0:T(8,128)(2,1)S(1)} %get-tuple-element.135.values_ref, ...), custom_call_target="tpu_custom_call" | custom-call | flops 4429185024 | bytes 2 | tf_op jit(solution)/shard_map/pallas_call | solution.py:243
  17.1 0.0 collective-permute-done.2.far_keys_ref
  17.1 0.0 collective-permute-done.5.refs_6_
  17.1 4.2 %shard_map.89 = (f32[512,1536]{1,0:T(8,128)S(1)}, bf16[12,512,256]{2,1,0:T(8,128)(2,1)S(1)}, s32[1]{0:T(128)}) custom-call(bf16[512,1536]{1,0:T(8,128)(2,1)S(1)} %copy-done, bf16[176,1536]{1,0:T(8,128)(2,1)S(1)} %get-tuple-element.136.sent_keys_ref, bf16[176,1536]{1,0:T(8,128)(2,1)S(1)} %collective-permute-done.2.far_keys_ref, ...), custom_call_target="tpu_custom_call" | custom-call | flops 553648128 | bytes 1572864 | tf_op jit(solution)/shard_map/pallas_call | solution.py:243
  22.0 0.0 collective-permute-done.6
  22.1 0.0 slice-done
  22.1 0.0 slice-done.1
  22.1 10.6 %conditional.1 = (bf16[512,1536]{1,0:T(8,128)(2,1)}) conditional(s32[]{:T(128)} %bitcast.2, (f32[512,1536]{1,0:T(8,128)S(1)}, bf16[12,512,256]{2,1,0:T(8,128)(2,1)S(1)}, bf16[176,1536]{1,0:T(8,128)(2,1)S(1)}, f32[1,1536]{1,0:T(1,128)S(1)}, bf16[1536,1536]{1,0:T(8,128)(2,1)S(1)}) %tuple.31, (bf16[512,1536]{1,0:T(8,128)(2,1)S(1)}, ...), branch_computations={%region_0.0_spmd, %region_1.0_spmd, %region_2.0_spmd} | conditional | flops 3674210304 | bytes 12976217 | solution.py:361
  22.3 5.4 %branch_1_fun.2 = (f32[512,1536]{1,0:T(8,128)S(1)}, bf16[12,512,256]{2,1,0:T(8,128)(2,1)S(1)}, s32[1]{0:T(128)}) custom-call(bf16[512,1536]{1,0:T(8,128)(2,1)S(1)} %get-tuple-element.82.queries_ref, bf16[176,1536]{1,0:T(8,128)(2,1)S(1)} %get-tuple-element.83.sent_keys_ref, bf16[176,1536]{1,0:T(8,128)(2,1)S(1)} %get-tuple-element.84.far_keys_ref, ...), custom_call_target="tpu_custom_call" | custom-call | flops 553648128 | bytes 1572864 | tf_op jit(solution)/shard_map/cond/branch_1_fun/pallas_call | solution.py:243
  27.7 4.9 %branch_1_fun.3 = bf16[512,1536]{1,0:T(8,128)(2,1)} custom-call(f32[512,1536]{1,0:T(8,128)S(1)} %get-tuple-element.93.accum_ref, bf16[12,512,256]{2,1,0:T(8,128)(2,1)S(1)} %get-tuple-element.94.weights_ref, bf16[176,1536]{1,0:T(8,128)(2,1)S(1)} %get-tuple-element.95.far_values_ref, f32[1,1536]{1,0:T(1,128)S(1)} %get-tuple-element.96.gain_ref, ...), custom_call_target="tpu_custom_call" | custom-call | flops 2818572288 | bytes 4718592 | tf_op jit(solution)/shard_map/cond/branch_1_fun/pallas_call | solution.py:243
  (2 shorter events, 0.0 us)
Async XLA Ops:
  0.0 5.2 %copy-start.1 = (s32[1,2,256]{2,1,0:T(2,128)S(1)}, s32[1,2,256]{2,1,0:T(2,128)}, u32[]{:S(2)}) copy-start(s32[1,2,256]{2,1,0:T(2,128)} %adjacency_ref.1) | copy-start | bytes 6148
  0.0 5.2 %copy-start.2 = (s32[4,2]{0,1:T(2,128)S(1)}, s32[4,2]{0,1:T(2,128)}, u32[]{:S(2)}) copy-start(s32[4,2]{0,1:T(2,128)} %param.17) | copy-start | bytes 100
  2.4 5.9 %copy-start.3 = (f32[1536]{0:T(1024)S(1)}, f32[1536]{0:T(1024)}, u32[]{:S(2)}) copy-start(f32[1536]{0:T(1024)} %param.14) | copy-start | bytes 18436
  2.4 5.9 %copy-start = (bf16[512,1536]{1,0:T(8,128)(2,1)S(1)}, bf16[512,1536]{1,0:T(8,128)(2,1)}, u32[]{:S(2)}) copy-start(bf16[512,1536]{1,0:T(8,128)(2,1)} %queries_ref.5) | copy-start | bytes 4718596
  2.4 5.9 %collective-permute-start.3 = (bf16[592,1536]{1,0:T(8,128)(2,1)S(1)}, bf16[592,1536]{1,0:T(8,128)(2,1)S(1)}, u32[]{:S(2)}, u32[]{:S(2)}) collective-permute-start(bf16[592,1536]{1,0:T(8,128)(2,1)S(1)} %get-tuple-element.137), channel_id=1, source_target_pairs={{0,1},{1,0},{2,3},{3,2},{4,5},{5,4},{6,7},{7,6},{8,9},{9,8},{10,11... | collective-permute-start | bytes 5455880 | tf_op jit(solution)/shard_map/ppermute | solution.py:266
  2.6 9.8 %collective-permute-start.4 = (bf16[64,1536]{1,0:T(8,128)(2,1)S(1)}, bf16[64,1536]{1,0:T(8,128)(2,1)S(1)}, u32[]{:S(2)}, u32[]{:S(2)}) collective-permute-start(bf16[64,1536]{1,0:T(8,128)(2,1)S(1)} %get-tuple-element.141.refs_4_), channel_id=1, source_target_pairs={{0,3},{1,2},{2,1},{3,0},{4,7},{5,6},{6,5},{7,4},{8,11},{9,10},{10,... | collective-permute-start | bytes 589832 | tf_op jit(solution)/shard_map/ppermute | solution.py:266
  6.5 10.6 %collective-permute-start.2 = (bf16[176,1536]{1,0:T(8,128)(2,1)S(1)}, bf16[176,1536]{1,0:T(8,128)(2,1)S(1)}, u32[]{:S(2)}, u32[]{:S(2)}) collective-permute-start(bf16[176,1536]{1,0:T(8,128)(2,1)S(1)} %get-tuple-element.136.sent_keys_ref), channel_id=1, source_target_pairs={{0,4},{1,2},{2,1},{3,7},{4,0},{5,6},{6,5},{7,3},{8,12},{9,10},{10,... | collective-permute-start | bytes 1622024 | tf_op jit(solution)/shard_map/ppermute | solution.py:276
  6.6 15.5 %collective-permute-start.6 = (bf16[176,1536]{1,0:T(8,128)(2,1)S(1)}, bf16[176,1536]{1,0:T(8,128)(2,1)S(1)}, u32[]{:S(2)}, u32[]{:S(2)}) collective-permute-start(bf16[176,1536]{1,0:T(8,128)(2,1)S(1)} %get-tuple-element.149), channel_id=1, source_target_pairs={{0,4},{1,2},{2,1},{3,7},{4,0},{5,6},{6,5},{7,3},{8,12},{9,10},{10,... | collective-permute-start | bytes 1622024 | tf_op jit(solution)/shard_map/ppermute | solution.py:276
  8.3 13.7 %slice-start = ((s8[4718592]{0:T(1024)(128)(4,1)}), s8[4194304]{0:T(1024)(128)(4,1)S(1)}, s32[]{:S(2)}) async-start(s8[4718592]{0:T(1024)(128)(4,1)} %bitcast.3), calls=%async_computation | async-start | bytes 8388608
  12.3 9.7 %slice-start.1 = ((s8[4718592]{0:T(1024)(128)(4,1)}), s8[524288]{0:T(1024)(128)(4,1)S(1)}, s32[]{:S(2)}) async-start(s8[4718592]{0:T(1024)(128)(4,1)} %bitcast.3), calls=%async_computation.1 | async-start | bytes 1048576
  12.4 4.8 %collective-permute-start.5 = (bf16[64,1536]{1,0:T(8,128)(2,1)S(1)}, bf16[64,1536]{1,0:T(8,128)(2,1)S(1)}, u32[]{:S(2)}, u32[]{:S(2)}) collective-permute-start(bf16[64,1536]{1,0:T(8,128)(2,1)S(1)} %collective-permute-done.4.refs_5_), channel_id=1, source_target_pairs={{0,1},{1,0},{2,3},{3,2},{4,5},{5,4},{6,7},{7,6},{8,9},{9,8},{10,11... | collective-permute-start | bytes 589832 | tf_op jit(solution)/shard_map/ppermute | solution.py:266
